TPU v7x, 512 devices: a whole 4x8x8 slice. The times are simulated.
512 devices in a mesh: ta: 16 (over y_hi, z), gz: 8 (over y_lo, core), yx: 4 (over x).
Axes of the slice: x: 4, y: 8 (y_hi: 2, y_lo: 4; y = y_hi * 4 + y_lo), z: 8, core: 2. Of those that a mesh axis runs over, the one named last changes fastest.
Arguments:
- source: bfloat16 [16, 8, 4, 12, 32, 128], P('ta', 'gz', 'yx'), may hold values from -180 to 180
- diag_block: bfloat16 [16, 8, 4, 12, 128, 128], P('ta', 'gz', 'yx'), may hold values from -2 to 7
- link_time: bfloat16 [16, 8, 4, 12, 128, 128], P('ta', 'gz', 'yx'), may hold values from -0.25 to 0.25
- link_zaxis: bfloat16 [16, 8, 4, 12, 128, 128], P('ta', 'gz', 'yx'), may hold values from -0.25 to 0.25
- link_yaxis: bfloat16 [16, 8, 4, 12, 128, 128], P('ta', 'gz', 'yx'), may hold values from -0.25 to 0.25
- link_xaxis: bfloat16 [16, 8, 4, 12, 128, 128], P('ta', 'gz', 'yx'), may hold values from -0.25 to 0.25
- prolong: bfloat16 [16, 8, 4, 12, 128, 128], P('ta', 'gz', 'yx'), may hold values from -0.375 to 0.375
- top_diag: bfloat16 [16, 8, 4, 128, 128], P('ta', 'gz', 'yx'), may hold values from -0.5 to 0.5
- top_time: bfloat16 [16, 8, 4, 128, 128], P('ta', 'gz', 'yx'), may hold values from -0.25 to 0.25
- top_zaxis: bfloat16 [16, 8, 4, 128, 128], P('ta', 'gz', 'yx'), may hold values from -0.25 to 0.25
- top_yaxis: bfloat16 [16, 8, 4, 128, 128], P('ta', 'gz', 'yx'), may hold values from -0.25 to 0.25
Outputs:
- update: float32 [16, 8, 4, 12, 32, 128], P('ta', 'gz', 'yx')
- remainder: float32 [16, 8, 4, 12, 32, 128], P('ta', 'gz', 'yx')
All inputs are finite; a program needn't handle non-finite values.
Results may differ from a plain program's by a relative error of at most 0.01.
Values may be sent and summed in bfloat16 or wider, within the bound.
A program may use at most 64 MiB of HBM per device.

v0:
```python
import jax
import jax.numpy as jnp
from jax import lax
from jax.sharding import PartitionSpec as P


def with_halo(value, sides, width):
    for axis, dim in sides:
        devices, length = (lax.axis_size(axis), value.shape[dim])
        up = [(i, (i + 1) % devices) for i in range(devices)]
        down = [(j, i) for i, j in up]
        last = lax.slice_in_dim(value, length - width, length, axis=dim)
        initial = lax.slice_in_dim(value, 0, width, axis=dim)
        before = lax.ppermute(last, axis, up)
        after = lax.ppermute(initial, axis, down)
        value = jnp.concatenate([before, value, after], axis=dim)
    return value


def passed_along(block, axis, distance):
    devices = range(lax.axis_size(axis))
    route = [((i - distance) % len(devices), i) for i in devices]
    return lax.ppermute(block, axis, route)


def multiply(blocks, vector_in):
    return jnp.einsum(
        "tzyxij,tzyxrj->tzyxri", blocks, vector_in, preferred_element_type=jnp.float32
    )


def transposed(blocks, vector_in):
    return jnp.einsum(
        "tzyxji,tzyxrj->tzyxri", blocks, vector_in, preferred_element_type=jnp.float32
    )


def coarse_mult(blocks, vector_in):
    return jnp.einsum(
        "tzyij,tzyrj->tzyri", blocks.astype(jnp.float32), vector_in, precision=lax.Precision.HIGHEST
    )


def coarse_trans(blocks, vector_in):
    return jnp.einsum(
        "tzyji,tzyrj->tzyri", blocks.astype(jnp.float32), vector_in, precision=lax.Precision.HIGHEST
    )


def without_last(array_in, dim_index):
    return lax.slice_in_dim(array_in, 0, array_in.shape[dim_index] - 1, axis=dim_index)


def window(padded, step_t, step_z, step_y, sizes_in):
    return padded[
        1 + step_t : 1 + step_t + sizes_in[0],
        1 + step_z : 1 + step_z + sizes_in[1],
        1 + step_y : 1 + step_y + sizes_in[2],
    ]


def body(
    source,
    diag_block,
    link_time,
    link_zaxis,
    link_yaxis,
    link_xaxis,
    prolong,
    top_diag,
    top_time,
    top_zaxis,
    top_yaxis,
):
    restricted = jnp.einsum(
        "tzyxij,tzyxri->rj", prolong, source, preferred_element_type=jnp.float32
    )
    restricted = restricted[None, None, None]
    stacked = jnp.stack(
        [
            restricted,
            coarse_trans(top_time, restricted),
            coarse_trans(top_zaxis, restricted),
            coarse_trans(top_yaxis, restricted),
        ],
        0,
    )
    coarse_pad = with_halo(stacked, (("ta", 1), ("gz", 2), ("yx", 3)), 1)
    correction = coarse_mult(top_diag, restricted)
    correction = (
        correction
        + coarse_mult(top_time, coarse_pad[0, 2:3, 1:2, 1:2])
        + coarse_pad[1, 0:1, 1:2, 1:2]
    )
    correction = (
        correction
        + coarse_mult(top_zaxis, coarse_pad[0, 1:2, 2:3, 1:2])
        + coarse_pad[2, 1:2, 0:1, 1:2]
    )
    correction = (
        correction
        + coarse_mult(top_yaxis, coarse_pad[0, 1:2, 1:2, 2:3])
        + coarse_pad[3, 1:2, 1:2, 0:1]
    )
    coarse_fix = correction.astype(jnp.bfloat16)[0, 0, 0]
    lifted = jnp.einsum(
        "tzyxij,rj->tzyxri", prolong, coarse_fix, preferred_element_type=jnp.float32
    ).astype(jnp.bfloat16)

    def local_terms(vector_in):
        summed = multiply(diag_block, vector_in) + multiply(link_xaxis, jnp.roll(vector_in, -1, 3))
        backed = transposed(link_xaxis, vector_in).astype(jnp.bfloat16)
        return summed + jnp.roll(backed, 1, 3).astype(jnp.float32)

    prior_time = jnp.concatenate([passed_along(link_time, "ta", 1), without_last(link_time, 0)], 0)
    prior_zaxis = jnp.concatenate(
        [passed_along(link_zaxis, "gz", 1), without_last(link_zaxis, 1)], 1
    )
    prior_yaxis = jnp.concatenate(
        [passed_along(link_yaxis, "yx", 1), without_last(link_yaxis, 2)], 2
    )

    def apply_dirac(vector_in):
        sizes_in = vector_in.shape
        padded = with_halo(vector_in, (("ta", 0), ("gz", 1), ("yx", 2)), 1)
        summed = local_terms(vector_in)
        summed = summed + multiply(link_time, window(padded, 1, 0, 0, sizes_in))
        summed = summed + transposed(prior_time, window(padded, -1, 0, 0, sizes_in)).astype(
            jnp.bfloat16
        ).astype(jnp.float32)
        summed = summed + multiply(link_zaxis, window(padded, 0, 1, 0, sizes_in))
        summed = summed + transposed(prior_zaxis, window(padded, 0, -1, 0, sizes_in)).astype(
            jnp.bfloat16
        ).astype(jnp.float32)
        summed = summed + multiply(link_yaxis, window(padded, 0, 0, 1, sizes_in))
        summed = summed + transposed(prior_yaxis, window(padded, 0, 0, -1, sizes_in)).astype(
            jnp.bfloat16
        ).astype(jnp.float32)
        return summed

    applied = apply_dirac(lifted)
    resid = (source.astype(jnp.float32) - applied).astype(jnp.bfloat16)
    image = apply_dirac(resid)
    resid_wide = resid.astype(jnp.float32)
    cross_term = jnp.sum(image * resid_wide, axis=(0, 1, 2, 3, 5))
    energy = jnp.sum(image * image, axis=(0, 1, 2, 3, 5))
    cross_term, energy = lax.psum((cross_term, energy), ("ta", "gz", "yx"))
    factor = cross_term / (energy + 1e-06)
    update = lifted.astype(jnp.float32) + factor[:, None] * resid_wide
    remainder = resid_wide - factor[:, None] * image
    return (update, remainder)


def solution(mesh):
    in_specs = (
        P("ta", "gz", "yx", None, None, None),
        P("ta", "gz", "yx", None, None, None),
        P("ta", "gz", "yx", None, None, None),
        P("ta", "gz", "yx", None, None, None),
        P("ta", "gz", "yx", None, None, None),
        P("ta", "gz", "yx", None, None, None),
        P("ta", "gz", "yx", None, None, None),
        P("ta", "gz", "yx", None, None),
        P("ta", "gz", "yx", None, None),
        P("ta", "gz", "yx", None, None),
        P("ta", "gz", "yx", None, None),
    )
    out_specs = (P("ta", "gz", "yx", None, None, None), P("ta", "gz", "yx", None, None, None))
    return jax.shard_map(body, mesh=mesh, in_specs=in_specs, out_specs=out_specs, check_vma=False)
```

profile of v0, /device:TPU:1, one launch (start us, length us, event | category | flops | bytes accessed | tf_op | source)
XLA Modules:
  0.0 286.2 jit_solution(1724394576449067266)
XLA Ops:
  3.6 16.8 %collective-permute-start = (f32[4,1,1,1,32,128]{5,4,3,2,1,0:T(8,128)S(1)}, f32[4,1,1,1,32,128]{5,4,3,2,1,0:T(8,128)S(1)}, u32[]{:S(2)}, u32[]{:S(2)}) collective-permute-start(f32[4,1,1,1,32,128]{5,4,3,2,1,0:T(8,128)S(1)} %pad_maximum_fusion.6), channel_id=1, source_target_pairs={{32,0},{64,32},{96,64},{128,96},{160,128},{192,160},{224,192},{256... | collective-permute-start | bytes 196616 | tf_op jit(solution)/shard_map/ppermute | solution.py:15
  20.4 1.9 collective-permute-start.1
  22.3 9.8 %collective-permute-done.1 = f32[4,1,1,1,32,128]{5,4,3,2,1,0:T(8,128)S(1)} collective-permute-done((f32[4,1,1,1,32,128]{5,4,3,2,1,0:T(8,128)S(1)}, f32[4,1,1,1,32,128]{5,4,3,2,1,0:T(8,128)S(1)}, u32[]{:S(2)}, u32[]{:S(2)}) %collective-permute-start.1) | collective-permute-done | bytes 65568 | tf_op jit(solution)/shard_map/ppermute | solution.py:14
  32.2 4.1 %collective-permute-start.2 = (f32[4,3,1,1,32,128]{5,4,3,2,1,0:T(8,128)S(1)}, f32[4,3,1,1,32,128]{5,4,3,2,1,0:T(8,128)S(1)}, u32[]{:S(2)}, u32[]{:S(2)}) collective-permute-start(f32[4,3,1,1,32,128]{5,4,3,2,1,0:T(8,128)S(1)} %pad_maximum_fusion.5), channel_id=1, source_target_pairs={{4,0},{8,4},{12,8},{16,12},{20,16},{24,20},{28,24},{0,28},{5,1},{9... | collective-permute-start | bytes 589832 | tf_op jit(solution)/shard_map/ppermute | solution.py:15
  36.3 2.1 collective-permute-start.3
  41.3 4.5 %collective-permute-start.4 = (f32[4,3,3,1,32,128]{5,4,3,2,1,0:T(8,128)S(1)}, f32[4,3,3,1,32,128]{5,4,3,2,1,0:T(8,128)S(1)}, u32[]{:S(2)}, u32[]{:S(2)}) collective-permute-start(f32[4,3,3,1,32,128]{5,4,3,2,1,0:T(8,128)S(1)} %pad_maximum_fusion.2), channel_id=1, source_target_pairs={{1,0},{2,1},{3,2},{0,3},{5,4},{6,5},{7,6},{4,7},{9,8},{10,9},{11,1... | collective-permute-start | bytes 1769480 | tf_op jit(solution)/shard_map/ppermute | solution.py:15
  45.8 1.9 collective-permute-start.14
  47.7 4.7 %collective-permute-start.11 = (bf16[1,1,1,12,128,128]{5,4,3,2,1,0:T(8,128)(2,1)S(1)}, bf16[1,1,1,12,128,128]{5,4,3,2,1,0:T(8,128)(2,1)S(1)}, u32[]{:S(2)}, u32[]{:S(2)}) collective-permute-start(bf16[1,1,1,12,128,128]{5,4,3,2,1,0:T(8,128)(2,1)S(1)} %copy-done.4), channel_id=1, source_target_pairs={{28,0},{0,4},{4,8},{8,12},{12,16},{16,20},{20,24},{24,28},{29,1},{... | collective-permute-start | bytes 1179656 | tf_op jit(solution)/shard_map/ppermute | solution.py:23
  52.4 1.9 collective-permute-start.8
  54.3 2.4 collective-permute-start.5
  57.2 14.2 %collective-permute-done.5 = f32[4,3,3,1,32,128]{5,4,3,2,1,0:T(8,128)S(1)} collective-permute-done((f32[4,3,3,1,32,128]{5,4,3,2,1,0:T(8,128)S(1)}, f32[4,3,3,1,32,128]{5,4,3,2,1,0:T(8,128)S(1)}, u32[]{:S(2)}, u32[]{:S(2)}) %collective-permute-start.5) | collective-permute-done | bytes 589856 | tf_op jit(solution)/shard_map/ppermute | solution.py:14
  71.9 9.1 %collective-permute-start.6 = (bf16[1,1,1,12,32,128]{5,4,3,2,1,0:T(8,128)(2,1)S(1)}, bf16[1,1,1,12,32,128]{5,4,3,2,1,0:T(8,128)(2,1)S(1)}, u32[]{:S(2)}, u32[]{:S(2)}) collective-permute-start(bf16[1,1,1,12,32,128]{5,4,3,2,1,0:T(8,128)(2,1)S(1)} %bitcast.194), channel_id=1, source_target_pairs={{32,0},{64,32},{96,64},{128,96},{160,128},{192,160},{224,192},{256... | collective-permute-start | bytes 294920 | tf_op jit(solution)/shard_map/ppermute | solution.py:15
  80.9 1.9 collective-permute-start.7
  83.4 8.9 %collective-permute-done.7 = bf16[1,1,1,12,32,128]{5,4,3,2,1,0:T(8,128)(2,1)S(1)} collective-permute-done((bf16[1,1,1,12,32,128]{5,4,3,2,1,0:T(8,128)(2,1)S(1)}, bf16[1,1,1,12,32,128]{5,4,3,2,1,0:T(8,128)(2,1)S(1)}, u32[]{:S(2)}, u32[]{:S(2)}) %collective-permute-start.7) | collective-permute-done | bytes 98336 | tf_op jit(solution)/shard_map/ppermute | solution.py:14
  92.4 6.4 %collective-permute-start.9 = (bf16[3,1,1,12,32,128]{5,4,3,2,1,0:T(8,128)(2,1)S(1)}, bf16[3,1,1,12,32,128]{5,4,3,2,1,0:T(8,128)(2,1)S(1)}, u32[]{:S(2)}, u32[]{:S(2)}) collective-permute-start(bf16[3,1,1,12,32,128]{5,4,3,2,1,0:T(8,128)(2,1)S(1)} %pad_maximum_fusion.3), channel_id=1, source_target_pairs={{4,0},{8,4},{12,8},{16,12},{20,16},{24,20},{28,24},{0,28},{5,1},{9... | collective-permute-start | bytes 884744 | tf_op jit(solution)/shard_map/ppermute | solution.py:15
  98.7 3.6 %collective-permute-start.10 = (bf16[3,1,1,12,32,128]{5,4,3,2,1,0:T(8,128)(2,1)S(1)}, bf16[3,1,1,12,32,128]{5,4,3,2,1,0:T(8,128)(2,1)S(1)}, u32[]{:S(2)}, u32[]{:S(2)}) collective-permute-start(bf16[3,1,1,12,32,128]{5,4,3,2,1,0:T(8,128)(2,1)S(1)} %pad_maximum_fusion.3), channel_id=1, source_target_pairs={{0,4},{4,8},{8,12},{12,16},{16,20},{20,24},{24,28},{28,0},{1,5},{5... | collective-permute-start | bytes 884744 | tf_op jit(solution)/shard_map/ppermute | solution.py:14
  102.4 2.4 collective-permute-done.9
  104.8 2.1 collective-permute-done.10
  107.0 4.0 %collective-permute-start.12 = (bf16[3,3,1,12,32,128]{5,4,3,2,1,0:T(8,128)(2,1)S(1)}, bf16[3,3,1,12,32,128]{5,4,3,2,1,0:T(8,128)(2,1)S(1)}, u32[]{:S(2)}, u32[]{:S(2)}) collective-permute-start(bf16[3,3,1,12,32,128]{5,4,3,2,1,0:T(8,128)(2,1)S(1)} %pad_maximum_fusion), channel_id=1, source_target_pairs={{1,0},{2,1},{3,2},{0,3},{5,4},{6,5},{7,6},{4,7},{9,8},{10,9},{11,1... | collective-permute-start | bytes 2654216 | tf_op jit(solution)/shard_map/ppermute | solution.py:15
  111.3 1.9 collective-permute-start.13
  114.0 13.2 %collective-permute-done.12 = bf16[3,3,1,12,32,128]{5,4,3,2,1,0:T(8,128)(2,1)S(1)} collective-permute-done((bf16[3,3,1,12,32,128]{5,4,3,2,1,0:T(8,128)(2,1)S(1)}, bf16[3,3,1,12,32,128]{5,4,3,2,1,0:T(8,128)(2,1)S(1)}, u32[]{:S(2)}, u32[]{:S(2)}) %collective-permute-start.12) | collective-permute-done | bytes 884768 | tf_op jit(solution)/shard_map/ppermute | solution.py:15
  127.5 4.9 %collective-permute-done.13 = bf16[3,3,1,12,32,128]{5,4,3,2,1,0:T(8,128)(2,1)S(1)} collective-permute-done((bf16[3,3,1,12,32,128]{5,4,3,2,1,0:T(8,128)(2,1)S(1)}, bf16[3,3,1,12,32,128]{5,4,3,2,1,0:T(8,128)(2,1)S(1)}, u32[]{:S(2)}, u32[]{:S(2)}) %collective-permute-start.13) | collective-permute-done | bytes 884768 | tf_op jit(solution)/shard_map/ppermute | solution.py:14
  132.9 1.9 collective-permute-start.15
  134.9 3.4 %collective-permute-start.16 = (bf16[1,1,1,12,32,128]{5,4,3,2,1,0:T(8,128)(2,1)S(1)}, bf16[1,1,1,12,32,128]{5,4,3,2,1,0:T(8,128)(2,1)S(1)}, u32[]{:S(2)}, u32[]{:S(2)}) collective-permute-start(bf16[1,1,1,12,32,128]{5,4,3,2,1,0:T(8,128)(2,1)S(1)} %fusion.14), channel_id=1, source_target_pairs={{0,32},{32,64},{64,96},{96,128},{128,160},{160,192},{192,224},{224... | collective-permute-start | bytes 294920 | tf_op jit(solution)/shard_map/ppermute | solution.py:14
  138.5 7.8 %collective-permute-done.16 = bf16[1,1,1,12,32,128]{5,4,3,2,1,0:T(8,128)(2,1)S(1)} collective-permute-done((bf16[1,1,1,12,32,128]{5,4,3,2,1,0:T(8,128)(2,1)S(1)}, bf16[1,1,1,12,32,128]{5,4,3,2,1,0:T(8,128)(2,1)S(1)}, u32[]{:S(2)}, u32[]{:S(2)}) %collective-permute-start.16) | collective-permute-done | bytes 98336 | tf_op jit(solution)/shard_map/ppermute | solution.py:14
  146.3 8.1 %collective-permute-start.17 = (bf16[3,1,1,12,32,128]{5,4,3,2,1,0:T(8,128)(2,1)S(1)}, bf16[3,1,1,12,32,128]{5,4,3,2,1,0:T(8,128)(2,1)S(1)}, u32[]{:S(2)}, u32[]{:S(2)}) collective-permute-start(bf16[3,1,1,12,32,128]{5,4,3,2,1,0:T(8,128)(2,1)S(1)} %pad_maximum_fusion.4), channel_id=1, source_target_pairs={{4,0},{8,4},{12,8},{16,12},{20,16},{24,20},{28,24},{0,28},{5,1},{9... | collective-permute-start | bytes 884744 | tf_op jit(solution)/shard_map/ppermute | solution.py:15
  154.4 2.1 collective-permute-start.18
  156.9 2.1 collective-permute-done.17
  159.0 2.5 collective-permute-done.18
  163.8 4.6 %collective-permute-start.19 = (bf16[3,3,1,12,32,128]{5,4,3,2,1,0:T(8,128)(2,1)S(1)}, bf16[3,3,1,12,32,128]{5,4,3,2,1,0:T(8,128)(2,1)S(1)}, u32[]{:S(2)}, u32[]{:S(2)}) collective-permute-start(bf16[3,3,1,12,32,128]{5,4,3,2,1,0:T(8,128)(2,1)S(1)} %pad_maximum_fusion.1), channel_id=1, source_target_pairs={{1,0},{2,1},{3,2},{0,3},{5,4},{6,5},{7,6},{4,7},{9,8},{10,9},{11,1... | collective-permute-start | bytes 2654216 | tf_op jit(solution)/shard_map/ppermute | solution.py:15
  169.1 13.5 %collective-permute-done.20 = bf16[3,3,1,12,32,128]{5,4,3,2,1,0:T(8,128)(2,1)S(1)} collective-permute-done((bf16[3,3,1,12,32,128]{5,4,3,2,1,0:T(8,128)(2,1)S(1)}, bf16[3,3,1,12,32,128]{5,4,3,2,1,0:T(8,128)(2,1)S(1)}, u32[]{:S(2)}, u32[]{:S(2)}) %collective-permute-start.20) | collective-permute-done | bytes 884768 | tf_op jit(solution)/shard_map/ppermute | solution.py:14
  184.8 100.6 %all-reduce = (f32[32]{0:T(128)S(1)}, f32[32]{0:T(128)S(1)}) all-reduce(f32[32]{0:T(128)S(1)} %get-tuple-element.6, f32[32]{0:T(128)S(1)} %multiply_reduce_fusion), channel_id=1, replica_groups=mesh['ta'=16,'gz'=8,'yx'=4] {'ta','gz','yx'}, use_global_device_ids=true, to_apply=%region_1.2 | all-reduce | flops 64 | bytes 512 | tf_op jit(solution)/shard_map/psum | solution.py:147
  (78 shorter events, 16.0 us)
Async XLA Ops:
  0.6 82.6 %copy-start = (bf16[1,1,1,12,128,128]{5,4,3,2,1,0:T(8,128)(2,1)S(1)}, bf16[1,1,1,12,128,128]{5,4,3,2,1,0:T(8,128)(2,1)}, u32[]{:S(2)}) copy-start(bf16[1,1,1,12,128,128]{5,4,3,2,1,0:T(8,128)(2,1)} %param.16) | copy-start | bytes 1179652
  0.6 1.3 copy-start.9
  1.9 0.8 copy-start.8
  2.7 0.8 copy-start.7
  3.6 18.7 %collective-permute-start = (f32[4,1,1,1,32,128]{5,4,3,2,1,0:T(8,128)S(1)}, f32[4,1,1,1,32,128]{5,4,3,2,1,0:T(8,128)S(1)}, u32[]{:S(2)}, u32[]{:S(2)}) collective-permute-start(f32[4,1,1,1,32,128]{5,4,3,2,1,0:T(8,128)S(1)} %pad_maximum_fusion.6), channel_id=1, source_target_pairs={{32,0},{64,32},{96,64},{128,96},{160,128},{192,160},{224,192},{256... | collective-permute-start | bytes 196616 | tf_op jit(solution)/shard_map/ppermute | solution.py:15
  20.4 11.7 %collective-permute-start.1 = (f32[4,1,1,1,32,128]{5,4,3,2,1,0:T(8,128)S(1)}, f32[4,1,1,1,32,128]{5,4,3,2,1,0:T(8,128)S(1)}, u32[]{:S(2)}, u32[]{:S(2)}) collective-permute-start(f32[4,1,1,1,32,128]{5,4,3,2,1,0:T(8,128)S(1)} %pad_maximum_fusion.6), channel_id=1, source_target_pairs={{0,32},{32,64},{64,96},{96,128},{128,160},{160,192},{192,224},{224... | collective-permute-start | bytes 196616 | tf_op jit(solution)/shard_map/ppermute | solution.py:14
  32.1 13.7 %copy-start.5 = (bf16[1,1,1,12,128,128]{5,4,3,2,1,0:T(8,128)(2,1)S(1)}, bf16[1,1,1,12,128,128]{5,4,3,2,1,0:T(8,128)(2,1)}, u32[]{:S(2)}) copy-start(bf16[1,1,1,12,128,128]{5,4,3,2,1,0:T(8,128)(2,1)} %param.15) | copy-start | bytes 1179652
  32.1 15.6 %copy-start.4 = (bf16[1,1,1,12,128,128]{5,4,3,2,1,0:T(8,128)(2,1)S(1)}, bf16[1,1,1,12,128,128]{5,4,3,2,1,0:T(8,128)(2,1)}, u32[]{:S(2)}) copy-start(bf16[1,1,1,12,128,128]{5,4,3,2,1,0:T(8,128)(2,1)} %param.14) | copy-start | bytes 1179652
  32.1 20.3 %copy-start.1 = (bf16[1,1,1,12,128,128]{5,4,3,2,1,0:T(8,128)(2,1)S(1)}, bf16[1,1,1,12,128,128]{5,4,3,2,1,0:T(8,128)(2,1)}, u32[]{:S(2)}) copy-start(bf16[1,1,1,12,128,128]{5,4,3,2,1,0:T(8,128)(2,1)} %param.13) | copy-start | bytes 1179652
  32.2 24.6 %copy-start.10 = (bf16[1,1,1,128,128]{4,3,2,1,0:T(8,128)(2,1)S(1)}, bf16[1,1,1,128,128]{4,3,2,1,0:T(8,128)(2,1)}, u32[]{:S(2)}) copy-start(bf16[1,1,1,128,128]{4,3,2,1,0:T(8,128)(2,1)} %param.18) | copy-start | bytes 98308
  32.2 7.6 %collective-permute-start.2 = (f32[4,3,1,1,32,128]{5,4,3,2,1,0:T(8,128)S(1)}, f32[4,3,1,1,32,128]{5,4,3,2,1,0:T(8,128)S(1)}, u32[]{:S(2)}, u32[]{:S(2)}) collective-permute-start(f32[4,3,1,1,32,128]{5,4,3,2,1,0:T(8,128)S(1)} %pad_maximum_fusion.5), channel_id=1, source_target_pairs={{4,0},{8,4},{12,8},{16,12},{20,16},{24,20},{28,24},{0,28},{5,1},{9... | collective-permute-start | bytes 589832 | tf_op jit(solution)/shard_map/ppermute | solution.py:15
  36.3 4.9 %collective-permute-start.3 = (f32[4,3,1,1,32,128]{5,4,3,2,1,0:T(8,128)S(1)}, f32[4,3,1,1,32,128]{5,4,3,2,1,0:T(8,128)S(1)}, u32[]{:S(2)}, u32[]{:S(2)}) collective-permute-start(f32[4,3,1,1,32,128]{5,4,3,2,1,0:T(8,128)S(1)} %pad_maximum_fusion.5), channel_id=1, source_target_pairs={{0,4},{4,8},{8,12},{12,16},{16,20},{20,24},{24,28},{28,0},{1,5},{5... | collective-permute-start | bytes 589832 | tf_op jit(solution)/shard_map/ppermute | solution.py:14
  41.2 30.4 %copy-start.2 = (bf16[1,1,1,12,128,128]{5,4,3,2,1,0:T(8,128)(2,1)S(1)}, bf16[1,1,1,12,128,128]{5,4,3,2,1,0:T(8,128)(2,1)}, u32[]{:S(2)}) copy-start(bf16[1,1,1,12,128,128]{5,4,3,2,1,0:T(8,128)(2,1)} %param.17) | copy-start | bytes 1179652
  41.3 15.8 %collective-permute-start.4 = (f32[4,3,3,1,32,128]{5,4,3,2,1,0:T(8,128)S(1)}, f32[4,3,3,1,32,128]{5,4,3,2,1,0:T(8,128)S(1)}, u32[]{:S(2)}, u32[]{:S(2)}) collective-permute-start(f32[4,3,3,1,32,128]{5,4,3,2,1,0:T(8,128)S(1)} %pad_maximum_fusion.2), channel_id=1, source_target_pairs={{1,0},{2,1},{3,2},{0,3},{5,4},{6,5},{7,6},{4,7},{9,8},{10,9},{11,1... | collective-permute-start | bytes 1769480 | tf_op jit(solution)/shard_map/ppermute | solution.py:15
  45.8 81.7 %collective-permute-start.14 = (bf16[1,1,1,12,128,128]{5,4,3,2,1,0:T(8,128)(2,1)S(1)}, bf16[1,1,1,12,128,128]{5,4,3,2,1,0:T(8,128)(2,1)S(1)}, u32[]{:S(2)}, u32[]{:S(2)}) collective-permute-start(bf16[1,1,1,12,128,128]{5,4,3,2,1,0:T(8,128)(2,1)S(1)} %copy-done.5), channel_id=1, source_target_pairs={{3,0},{0,1},{1,2},{2,3},{7,4},{4,5},{5,6},{6,7},{11,8},{8,9},{9,10... | collective-permute-start | bytes 1179656 | tf_op jit(solution)/shard_map/ppermute | solution.py:23
  47.7 66.0 %collective-permute-start.11 = (bf16[1,1,1,12,128,128]{5,4,3,2,1,0:T(8,128)(2,1)S(1)}, bf16[1,1,1,12,128,128]{5,4,3,2,1,0:T(8,128)(2,1)S(1)}, u32[]{:S(2)}, u32[]{:S(2)}) collective-permute-start(bf16[1,1,1,12,128,128]{5,4,3,2,1,0:T(8,128)(2,1)S(1)} %copy-done.4), channel_id=1, source_target_pairs={{28,0},{0,4},{4,8},{8,12},{12,16},{16,20},{20,24},{24,28},{29,1},{... | collective-permute-start | bytes 1179656 | tf_op jit(solution)/shard_map/ppermute | solution.py:23
  52.4 60.8 %collective-permute-start.8 = (bf16[1,1,1,12,128,128]{5,4,3,2,1,0:T(8,128)(2,1)S(1)}, bf16[1,1,1,12,128,128]{5,4,3,2,1,0:T(8,128)(2,1)S(1)}, u32[]{:S(2)}, u32[]{:S(2)}) collective-permute-start(bf16[1,1,1,12,128,128]{5,4,3,2,1,0:T(8,128)(2,1)S(1)} %copy-done.1), channel_id=1, source_target_pairs={{480,0},{0,32},{32,64},{64,96},{96,128},{128,160},{160,192},{192,2... | collective-permute-start | bytes 1179656 | tf_op jit(solution)/shard_map/ppermute | solution.py:23
  54.3 17.1 %collective-permute-start.5 = (f32[4,3,3,1,32,128]{5,4,3,2,1,0:T(8,128)S(1)}, f32[4,3,3,1,32,128]{5,4,3,2,1,0:T(8,128)S(1)}, u32[]{:S(2)}, u32[]{:S(2)}) collective-permute-start(f32[4,3,3,1,32,128]{5,4,3,2,1,0:T(8,128)S(1)} %pad_maximum_fusion.2), channel_id=1, source_target_pairs={{0,1},{1,2},{2,3},{3,0},{4,5},{5,6},{6,7},{7,4},{8,9},{9,10},{10,1... | collective-permute-start | bytes 1769480 | tf_op jit(solution)/shard_map/ppermute | solution.py:14
  56.9 26.0 %copy-start.3 = (bf16[1,1,1,12,128,128]{5,4,3,2,1,0:T(8,128)(2,1)S(1)}, bf16[1,1,1,12,128,128]{5,4,3,2,1,0:T(8,128)(2,1)}, u32[]{:S(2)}) copy-start(bf16[1,1,1,12,128,128]{5,4,3,2,1,0:T(8,128)(2,1)} %param.12) | copy-start | bytes 1179652
  71.9 11.5 %collective-permute-start.6 = (bf16[1,1,1,12,32,128]{5,4,3,2,1,0:T(8,128)(2,1)S(1)}, bf16[1,1,1,12,32,128]{5,4,3,2,1,0:T(8,128)(2,1)S(1)}, u32[]{:S(2)}, u32[]{:S(2)}) collective-permute-start(bf16[1,1,1,12,32,128]{5,4,3,2,1,0:T(8,128)(2,1)S(1)} %bitcast.194), channel_id=1, source_target_pairs={{32,0},{64,32},{96,64},{128,96},{160,128},{192,160},{224,192},{256... | collective-permute-start | bytes 294920 | tf_op jit(solution)/shard_map/ppermute | solution.py:15
  80.9 11.4 %collective-permute-start.7 = (bf16[1,1,1,12,32,128]{5,4,3,2,1,0:T(8,128)(2,1)S(1)}, bf16[1,1,1,12,32,128]{5,4,3,2,1,0:T(8,128)(2,1)S(1)}, u32[]{:S(2)}, u32[]{:S(2)}) collective-permute-start(bf16[1,1,1,12,32,128]{5,4,3,2,1,0:T(8,128)(2,1)S(1)} %bitcast.195), channel_id=1, source_target_pairs={{0,32},{32,64},{64,96},{96,128},{128,160},{160,192},{192,224},{224... | collective-permute-start | bytes 294920 | tf_op jit(solution)/shard_map/ppermute | solution.py:14
  92.4 12.4 %collective-permute-start.9 = (bf16[3,1,1,12,32,128]{5,4,3,2,1,0:T(8,128)(2,1)S(1)}, bf16[3,1,1,12,32,128]{5,4,3,2,1,0:T(8,128)(2,1)S(1)}, u32[]{:S(2)}, u32[]{:S(2)}) collective-permute-start(bf16[3,1,1,12,32,128]{5,4,3,2,1,0:T(8,128)(2,1)S(1)} %pad_maximum_fusion.3), channel_id=1, source_target_pairs={{4,0},{8,4},{12,8},{16,12},{20,16},{24,20},{28,24},{0,28},{5,1},{9... | collective-permute-start | bytes 884744 | tf_op jit(solution)/shard_map/ppermute | solution.py:15
  98.7 8.2 %collective-permute-start.10 = (bf16[3,1,1,12,32,128]{5,4,3,2,1,0:T(8,128)(2,1)S(1)}, bf16[3,1,1,12,32,128]{5,4,3,2,1,0:T(8,128)(2,1)S(1)}, u32[]{:S(2)}, u32[]{:S(2)}) collective-permute-start(bf16[3,1,1,12,32,128]{5,4,3,2,1,0:T(8,128)(2,1)S(1)} %pad_maximum_fusion.3), channel_id=1, source_target_pairs={{0,4},{4,8},{8,12},{12,16},{16,20},{20,24},{24,28},{28,0},{1,5},{5... | collective-permute-start | bytes 884744 | tf_op jit(solution)/shard_map/ppermute | solution.py:14
  107.0 20.2 %collective-permute-start.12 = (bf16[3,3,1,12,32,128]{5,4,3,2,1,0:T(8,128)(2,1)S(1)}, bf16[3,3,1,12,32,128]{5,4,3,2,1,0:T(8,128)(2,1)S(1)}, u32[]{:S(2)}, u32[]{:S(2)}) collective-permute-start(bf16[3,3,1,12,32,128]{5,4,3,2,1,0:T(8,128)(2,1)S(1)} %pad_maximum_fusion), channel_id=1, source_target_pairs={{1,0},{2,1},{3,2},{0,3},{5,4},{6,5},{7,6},{4,7},{9,8},{10,9},{11,1... | collective-permute-start | bytes 2654216 | tf_op jit(solution)/shard_map/ppermute | solution.py:15
  111.3 21.1 %collective-permute-start.13 = (bf16[3,3,1,12,32,128]{5,4,3,2,1,0:T(8,128)(2,1)S(1)}, bf16[3,3,1,12,32,128]{5,4,3,2,1,0:T(8,128)(2,1)S(1)}, u32[]{:S(2)}, u32[]{:S(2)}) collective-permute-start(bf16[3,3,1,12,32,128]{5,4,3,2,1,0:T(8,128)(2,1)S(1)} %pad_maximum_fusion), channel_id=1, source_target_pairs={{0,1},{1,2},{2,3},{3,0},{4,5},{5,6},{6,7},{7,4},{8,9},{9,10},{10,1... | collective-permute-start | bytes 2654216 | tf_op jit(solution)/shard_map/ppermute | solution.py:14
  127.5 5.1 %copy-start.6 = (bf16[1,1,1,12,32,128]{5,4,3,2,1,0:T(8,128)(2,1)S(1)}, bf16[1,1,1,12,32,128]{5,4,3,2,1,0:T(8,128)(2,1)}, u32[]{:S(2)}) copy-start(bf16[1,1,1,12,32,128]{5,4,3,2,1,0:T(8,128)(2,1)} %param.11) | copy-start | bytes 294916
  132.9 5.5 %collective-permute-start.15 = (bf16[1,1,1,12,32,128]{5,4,3,2,1,0:T(8,128)(2,1)S(1)}, bf16[1,1,1,12,32,128]{5,4,3,2,1,0:T(8,128)(2,1)S(1)}, u32[]{:S(2)}, u32[]{:S(2)}) collective-permute-start(bf16[1,1,1,12,32,128]{5,4,3,2,1,0:T(8,128)(2,1)S(1)} %fusion.14), channel_id=1, source_target_pairs={{32,0},{64,32},{96,64},{128,96},{160,128},{192,160},{224,192},{256... | collective-permute-start | bytes 294920 | tf_op jit(solution)/shard_map/ppermute | solution.py:15
  134.9 11.4 %collective-permute-start.16 = (bf16[1,1,1,12,32,128]{5,4,3,2,1,0:T(8,128)(2,1)S(1)}, bf16[1,1,1,12,32,128]{5,4,3,2,1,0:T(8,128)(2,1)S(1)}, u32[]{:S(2)}, u32[]{:S(2)}) collective-permute-start(bf16[1,1,1,12,32,128]{5,4,3,2,1,0:T(8,128)(2,1)S(1)} %fusion.14), channel_id=1, source_target_pairs={{0,32},{32,64},{64,96},{96,128},{128,160},{160,192},{192,224},{224... | collective-permute-start | bytes 294920 | tf_op jit(solution)/shard_map/ppermute | solution.py:14
  146.3 12.7 %collective-permute-start.17 = (bf16[3,1,1,12,32,128]{5,4,3,2,1,0:T(8,128)(2,1)S(1)}, bf16[3,1,1,12,32,128]{5,4,3,2,1,0:T(8,128)(2,1)S(1)}, u32[]{:S(2)}, u32[]{:S(2)}) collective-permute-start(bf16[3,1,1,12,32,128]{5,4,3,2,1,0:T(8,128)(2,1)S(1)} %pad_maximum_fusion.4), channel_id=1, source_target_pairs={{4,0},{8,4},{12,8},{16,12},{20,16},{24,20},{28,24},{0,28},{5,1},{9... | collective-permute-start | bytes 884744 | tf_op jit(solution)/shard_map/ppermute | solution.py:15
  154.4 7.0 %collective-permute-start.18 = (bf16[3,1,1,12,32,128]{5,4,3,2,1,0:T(8,128)(2,1)S(1)}, bf16[3,1,1,12,32,128]{5,4,3,2,1,0:T(8,128)(2,1)S(1)}, u32[]{:S(2)}, u32[]{:S(2)}) collective-permute-start(bf16[3,1,1,12,32,128]{5,4,3,2,1,0:T(8,128)(2,1)S(1)} %pad_maximum_fusion.4), channel_id=1, source_target_pairs={{0,4},{4,8},{8,12},{12,16},{16,20},{20,24},{24,28},{28,0},{1,5},{5... | collective-permute-start | bytes 884744 | tf_op jit(solution)/shard_map/ppermute | solution.py:14
  161.5 21.1 %collective-permute-start.20 = (bf16[3,3,1,12,32,128]{5,4,3,2,1,0:T(8,128)(2,1)S(1)}, bf16[3,3,1,12,32,128]{5,4,3,2,1,0:T(8,128)(2,1)S(1)}, u32[]{:S(2)}, u32[]{:S(2)}) collective-permute-start(bf16[3,3,1,12,32,128]{5,4,3,2,1,0:T(8,128)(2,1)S(1)} %pad_maximum_fusion.1), channel_id=1, source_target_pairs={{0,1},{1,2},{2,3},{3,0},{4,5},{5,6},{6,7},{7,4},{8,9},{9,10},{10,1... | collective-permute-start | bytes 2654216 | tf_op jit(solution)/shard_map/ppermute | solution.py:14
  163.8 20.1 %collective-permute-start.19 = (bf16[3,3,1,12,32,128]{5,4,3,2,1,0:T(8,128)(2,1)S(1)}, bf16[3,3,1,12,32,128]{5,4,3,2,1,0:T(8,128)(2,1)S(1)}, u32[]{:S(2)}, u32[]{:S(2)}) collective-permute-start(bf16[3,3,1,12,32,128]{5,4,3,2,1,0:T(8,128)(2,1)S(1)} %pad_maximum_fusion.1), channel_id=1, source_target_pairs={{1,0},{2,1},{3,2},{0,3},{5,4},{6,5},{7,6},{4,7},{9,8},{10,9},{11,1... | collective-permute-start | bytes 2654216 | tf_op jit(solution)/shard_map/ppermute | solution.py:15
where the time goes:
time: 287 us; the launch traced here: 286 us
  blocking collectives  101 us (35%)
  starting transfers between devices  89.1 us (31%)
  waiting for transfers between devices  85.2 us (30%)
  matrix products  7.42 us (3%)
    psum x1, blocking collectives, body(): cross_term, energy = lax.psum((cross_term, energy), ('ta', 'gz', 'yx'))  101 us
    ppermute x9, waiting for transfers between devices, with_halo(): before = lax.ppermute(last, axis, up)  65 us
    ppermute x9, starting transfers between devices, with_halo(): after = lax.ppermute(initial, axis, down)  59.4 us
    ppermute x9, starting transfers between devices, with_halo(): before = lax.ppermute(last, axis, up)  21.2 us
    ppermute x9, waiting for transfers between devices, with_halo(): after = lax.ppermute(initial, axis, down)  20.2 us
    ppermute x3, starting transfers between devices, passed_along(): return lax.ppermute(block, axis, route)  8.51 us
  transfers between devices with their start and end apart: 21, of which 14 were waited for; matrix products, arithmetic and copies ran while one was open for 2% of the time, Pallas kernels for 0%

commit v1 on v0

v1 whole, which is shorter than its diff:
```python
import itertools

import jax
import jax.numpy as jnp
from jax import lax
from jax.experimental import pallas as pl
from jax.experimental.pallas import tpu as pltpu
from jax.sharding import PartitionSpec as P

MESH = pl.DeviceIdType.MESH
F32 = jnp.float32
BF16 = jnp.bfloat16

NX, RHS, DOF = 12, 32, 128
CHUNKS = 2
SPAN = NX // CHUNKS
SIZES = {"core": 2, "x": 4, "y": 8, "z": 8}
PHASES = (("core", "x"), ("y",), ("z",))


def offsets_of(phase):
    every = itertools.product(*(range(SIZES[axis]) for axis in phase))
    return [dict(zip(phase, step)) for step in every if any(step)]


COUNTS = [len(offsets_of(phase)) for phase in PHASES]


def forward(vector, block):
    return lax.dot_general(vector, block, (((1,), (1,)), ((), ())), preferred_element_type=F32)


def adjoint(vector, block):
    return lax.dot_general(vector, block, (((1,), (0,)), ((), ())), preferred_element_type=F32)


def halves(value):
    high = value.astype(BF16)
    low = (value - high.astype(F32)).astype(BF16)
    return jnp.concatenate([high, low], axis=0)


def fold(value):
    return value[:RHS] + value[RHS:]


def kernel(
    src_h, diag_h, lt_h, lz_h, ly_h, lx_h, pro_h, td_h, tt_h, tz_h, ty_h,
    lifted_o, resid_o, image_o, factor_o,
    src, diag, links, pro, tops,
    field, back, field_in, back_in, total, image, factor,
    coarse, coarse_in, hop_in,
    sum_out, sum_in,
    load_sem, store_sem,
    coarse_send, coarse_recv, field_send, field_recv, back_send, back_recv,
    sum_send, sum_recv,
):
    ta, gz, yx = lax.axis_index("ta"), lax.axis_index("gz"), lax.axis_index("yx")

    def at(ta_at, gz_at, yx_at):
        return (ta_at, gz_at, yx_at)

    plus = (
        at(lax.rem(ta + 1, 16), gz, yx),
        at(ta, lax.rem(gz + 1, 8), yx),
        at(ta, gz, lax.rem(yx + 1, 4)),
    )
    minus = (
        at(lax.rem(ta + 15, 16), gz, yx),
        at(ta, lax.rem(gz + 7, 8), yx),
        at(ta, gz, lax.rem(yx + 3, 4)),
    )
    here = {
        "core": lax.rem(gz, 2),
        "x": yx,
        "y": (ta // 8) * 4 + gz // 2,
        "z": lax.rem(ta, 8),
    }

    def partner(step):
        place = {
            axis: lax.rem(here[axis] + step.get(axis, 0), size) if step.get(axis, 0) else here[axis]
            for axis, size in SIZES.items()
        }
        return at(
            (place["y"] // 4) * 8 + place["z"],
            lax.rem(place["y"], 4) * 2 + place["core"],
            place["x"],
        )

    loads = {}
    pairs = (
        ("pro", pro_h, pro),
        ("src", src_h, src),
        ("tt", tt_h, tops.at[0]),
        ("tz", tz_h, tops.at[1]),
        ("ty", ty_h, tops.at[2]),
        ("td", td_h, tops.at[3]),
        ("lt", lt_h, links.at[0]),
        ("lz", lz_h, links.at[1]),
        ("ly", ly_h, links.at[2]),
        ("lx", lx_h, links.at[3]),
        ("diag", diag_h, diag),
    )
    for index, (name, source, target) in enumerate(pairs):
        loads[name] = pltpu.make_async_copy(source, target, load_sem.at[index])
        loads[name].start()

    barrier = pltpu.get_barrier_semaphore()
    greeted = list(plus) + list(minus)
    for phase in PHASES:
        greeted += [partner(step) for step in offsets_of(phase)]
    for device in greeted:
        pl.semaphore_signal(barrier, inc=1, device_id=device, device_id_type=MESH)

    def remote(source, target, send, recv, device):
        return pltpu.make_async_remote_copy(
            src_ref=source, dst_ref=target, send_sem=send, recv_sem=recv,
            device_id=device, device_id_type=MESH,
        )

    loads["pro"].wait()
    loads["src"].wait()
    restricted = adjoint(src[0], pro[0])
    for n in range(1, NX):
        restricted += adjoint(src[n], pro[n])
    coarse[0] = restricted
    split = halves(restricted)
    for mu, name in enumerate(("tt", "tz", "ty")):
        loads[name].wait()
        coarse[1 + mu] = fold(adjoint(split, tops[mu]))

    pl.semaphore_wait(barrier, len(greeted))

    coarse_copies = []
    for mu in range(3):
        coarse_copies.append(
            remote(coarse.at[0], coarse_in.at[mu], coarse_send.at[mu], coarse_recv.at[mu], minus[mu])
        )
        coarse_copies.append(
            remote(coarse.at[1 + mu], hop_in.at[mu], coarse_send.at[3 + mu], coarse_recv.at[3 + mu], plus[mu])
        )
    for copy in coarse_copies:
        copy.start()
    loads["td"].wait()
    correction = fold(forward(split, tops[3]))
    for mu in (2, 1, 0):
        coarse_copies[2 * mu].wait_recv()
        correction += fold(forward(halves(coarse_in[mu]), tops[mu]))
        coarse_copies[2 * mu + 1].wait_recv()
        correction += hop_in[mu]
    coarse_fix = correction.astype(BF16)

    def span(part):
        return pl.ds(part * SPAN, SPAN)

    def field_copy(turn, mu, part):
        return remote(
            field.at[turn, span(part)], field_in.at[turn, mu, span(part)],
            field_send.at[turn, mu, part], field_recv.at[turn, mu, part], minus[mu],
        )

    def back_copy(turn, mu, part):
        return remote(
            back.at[turn, mu, span(part)], back_in.at[turn, mu, span(part)],
            back_send.at[turn, mu, part], back_recv.at[turn, mu, part], plus[mu],
        )

    def sites(part):
        return range(part * SPAN, (part + 1) * SPAN)

    def send_field(turn, part):
        for mu in range(3):
            field_copy(turn, mu, part).start()

    def send_back(turn, mu, part):
        for n in sites(part):
            back[turn, mu, n] = adjoint(field[turn, n], links[mu, n]).astype(BF16)
        back_copy(turn, mu, part).start()

    def local_terms(turn):
        for n in range(NX):
            after, before = (n + 1) % NX, (n - 1) % NX
            value = forward(field[turn, n], diag[n])
            value += forward(field[turn, after], links[3, n])
            value += adjoint(field[turn, before], links[3, before]).astype(BF16).astype(F32)
            total[n] = value

    def arrived(turn, mu, part):
        field_copy(turn, mu, part).wait_recv()
        back_copy(turn, mu, part).wait_recv()

    def hop_terms(turn, mu, n):
        return forward(field_in[turn, mu, n], links[mu, n]) + back_in[turn, mu, n].astype(F32)

    def near_terms(turn):
        for mu in (2, 1):
            for part in range(CHUNKS):
                arrived(turn, mu, part)
                for n in sites(part):
                    total[n] += hop_terms(turn, mu, n)

    for part in range(CHUNKS):
        for n in sites(part):
            field[0, n] = forward(coarse_fix, pro[n]).astype(BF16)
        send_field(0, part)
    for mu, name in enumerate(("lt", "lz", "ly")):
        loads[name].wait()
        for part in range(CHUNKS):
            send_back(0, mu, part)
    store_lifted = pltpu.make_async_copy(field.at[0], lifted_o, store_sem.at[0])
    store_lifted.start()
    loads["lx"].wait()
    loads["diag"].wait()
    local_terms(0)
    near_terms(0)
    for part in range(CHUNKS):
        arrived(0, 0, part)
        for n in sites(part):
            applied = total[n] + hop_terms(0, 0, n)
            field[1, n] = (src[n].astype(F32) - applied).astype(BF16)
        send_field(1, part)
        send_back(1, 0, part)
    for mu in (1, 2):
        for part in range(CHUNKS):
            send_back(1, mu, part)
    store_resid = pltpu.make_async_copy(field.at[1], resid_o, store_sem.at[1])
    store_resid.start()

    local_terms(1)
    near_terms(1)
    cross = jnp.zeros((RHS, DOF), F32)
    energy = jnp.zeros((RHS, DOF), F32)
    for part in range(CHUNKS):
        arrived(1, 0, part)
        for n in sites(part):
            value = total[n] + hop_terms(1, 0, n)
            image[n] = value
            cross += value * field[1, n].astype(F32)
            energy += value * value
    store_image = pltpu.make_async_copy(image, image_o, store_sem.at[2])
    store_image.start()

    row = lax.broadcasted_iota(jnp.int32, (RHS, DOF), 0)
    lane = lax.broadcasted_iota(jnp.int32, (RHS, DOF), 1)
    cross_at = jnp.sum(cross, axis=1, keepdims=True)
    energy_at = jnp.sum(energy, axis=1, keepdims=True)
    laid = jnp.where(lane == row, cross_at, jnp.where(lane == row + RHS, energy_at, 0.0))
    sums = jnp.sum(laid, axis=0, keepdims=True)

    base = 0
    for index, phase in enumerate(PHASES):
        sum_out[index] = sums
        copies = []
        for slot, step in enumerate(offsets_of(phase)):
            copies.append(
                remote(
                    sum_out.at[index], sum_in.at[base + slot],
                    sum_send.at[base + slot], sum_recv.at[base + slot], partner(step),
                )
            )
        for copy in copies:
            copy.start()
        for copy in copies:
            copy.wait_recv()
        for slot in range(len(copies)):
            sums = sums + sum_in[base + slot]
        for copy in copies:
            copy.wait_send()
        base += len(copies)

    wide = jnp.broadcast_to(sums, (RHS, DOF))
    cross_sum = jnp.sum(jnp.where(lane == row, wide, 0.0), axis=1, keepdims=True)
    energy_sum = jnp.sum(jnp.where(lane == row + RHS, wide, 0.0), axis=1, keepdims=True)
    factor[...] = jnp.broadcast_to(cross_sum / (energy_sum + 1e-06), (RHS, DOF))
    store_factor = pltpu.make_async_copy(factor, factor_o, store_sem.at[3])
    store_factor.start()

    for copy in coarse_copies:
        copy.wait_send()
    for turn in range(2):
        for mu in range(3):
            for part in range(CHUNKS):
                field_copy(turn, mu, part).wait_send()
                back_copy(turn, mu, part).wait_send()
    for copy in (store_lifted, store_resid, store_image, store_factor):
        copy.wait()


def body(source, diag_block, link_time, link_zaxis, link_yaxis, link_xaxis, prolong,
         top_diag, top_time, top_zaxis, top_yaxis):
    shape = source.shape
    blocks = [
        value.reshape(NX, DOF, DOF)
        for value in (diag_block, link_time, link_zaxis, link_yaxis, link_xaxis, prolong)
    ]
    tops = [value.reshape(DOF, DOF) for value in (top_diag, top_time, top_zaxis, top_yaxis)]
    vmem, dma = pltpu.VMEM, pltpu.SemaphoreType.DMA
    total = sum(COUNTS)
    lifted, resid, image, factor = pl.pallas_call(
        kernel,
        out_shape=(
            jax.ShapeDtypeStruct((NX, RHS, DOF), BF16),
            jax.ShapeDtypeStruct((NX, RHS, DOF), BF16),
            jax.ShapeDtypeStruct((NX, RHS, DOF), F32),
            jax.ShapeDtypeStruct((RHS, DOF), F32),
        ),
        in_specs=[pl.BlockSpec(memory_space=pl.ANY)] * 11,
        out_specs=[pl.BlockSpec(memory_space=pl.ANY)] * 4,
        scratch_shapes=[
            vmem((NX, RHS, DOF), BF16),
            vmem((NX, DOF, DOF), BF16),
            vmem((4, NX, DOF, DOF), BF16),
            vmem((NX, DOF, DOF), BF16),
            vmem((4, DOF, DOF), BF16),
            vmem((2, NX, RHS, DOF), BF16),
            vmem((2, 3, NX, RHS, DOF), BF16),
            vmem((2, 3, NX, RHS, DOF), BF16),
            vmem((2, 3, NX, RHS, DOF), BF16),
            vmem((NX, RHS, DOF), F32),
            vmem((NX, RHS, DOF), F32),
            vmem((RHS, DOF), F32),
            vmem((4, RHS, DOF), F32),
            vmem((3, RHS, DOF), F32),
            vmem((3, RHS, DOF), F32),
            vmem((len(PHASES), 1, DOF), F32),
            vmem((total, 1, DOF), F32),
            dma((11,)),
            dma((4,)),
            dma((6,)),
            dma((6,)),
            dma((2, 3, CHUNKS)),
            dma((2, 3, CHUNKS)),
            dma((2, 3, CHUNKS)),
            dma((2, 3, CHUNKS)),
            dma((total,)),
            dma((total,)),
        ],
        compiler_params=pltpu.CompilerParams(
            collective_id=0, has_side_effects=True, vmem_limit_bytes=32 * 1024 * 1024
        ),
        name="smooth",
    )(source.reshape(NX, RHS, DOF), *blocks, *tops)
    wide = resid.astype(F32)
    update = lifted.astype(F32) + factor * wide
    remainder = wide - factor * image
    return update.reshape(shape), remainder.reshape(shape)


def solution(mesh):
    field = P("ta", "gz", "yx", None, None, None)
    top = P("ta", "gz", "yx", None, None)
    return jax.shard_map(
        body, mesh=mesh, in_specs=(field,) * 7 + (top,) * 4, out_specs=(field, field), check_vma=False
    )
```

time: 287 us -> 66.5 us (0.23)
  the two profiles are of different devices: /device:TPU:1 before, /device:TPU:8 now
where the time goes in v1:
time: 66.5 us; the launch traced here: 65.9 us
  Pallas kernels  54.5 us (82%)
  local copies, waits for them, and re-layouts  9.89 us (15%)
  other arithmetic  0.79 us (1%)
    pallas_call x1, Pallas kernels, body(): pl.pallas_call(kernel, out_shape=(jax.ShapeDtypeStruct((NX, RHS, DOF), BF...  54.5 us
    unnamed x22, local copies, waits for them, and re-layouts  9.89 us

profile of v1, /device:TPU:8, one launch (start us, length us, event | category | flops | bytes accessed | tf_op | source)
XLA Modules:
  0.0 65.9 jit_solution(3534568333129433265)
XLA Ops:
  0.6 0.0 copy-start
  0.6 1.0 %copy-done = bf16[1,1,1,12,128,128]{5,4,3,2,1,0:T(8,128)(2,1)S(1)} copy-done((bf16[1,1,1,12,128,128]{5,4,3,2,1,0:T(8,128)(2,1)S(1)}, bf16[1,1,1,12,128,128]{5,4,3,2,1,0:T(8,128)(2,1)}, u32[]{:S(2)}) %copy-start) | copy-done | bytes 393240
  1.6 0.0 copy-start.1
  1.6 1.0 %copy-done.1 = bf16[1,1,1,12,128,128]{5,4,3,2,1,0:T(8,128)(2,1)S(1)} copy-done((bf16[1,1,1,12,128,128]{5,4,3,2,1,0:T(8,128)(2,1)S(1)}, bf16[1,1,1,12,128,128]{5,4,3,2,1,0:T(8,128)(2,1)}, u32[]{:S(2)}) %copy-start.1) | copy-done | bytes 393240
  2.6 0.0 copy-start.2
  2.6 1.0 %copy-done.2 = bf16[1,1,1,12,128,128]{5,4,3,2,1,0:T(8,128)(2,1)S(1)} copy-done((bf16[1,1,1,12,128,128]{5,4,3,2,1,0:T(8,128)(2,1)S(1)}, bf16[1,1,1,12,128,128]{5,4,3,2,1,0:T(8,128)(2,1)}, u32[]{:S(2)}) %copy-start.2) | copy-done | bytes 393240
  3.6 0.0 copy-start.3
  3.6 1.0 %copy-done.3 = bf16[1,1,1,12,128,128]{5,4,3,2,1,0:T(8,128)(2,1)S(1)} copy-done((bf16[1,1,1,12,128,128]{5,4,3,2,1,0:T(8,128)(2,1)S(1)}, bf16[1,1,1,12,128,128]{5,4,3,2,1,0:T(8,128)(2,1)}, u32[]{:S(2)}) %copy-start.3) | copy-done | bytes 393240
  4.6 0.0 copy-start.4
  4.6 1.0 %copy-done.4 = bf16[1,1,1,12,128,128]{5,4,3,2,1,0:T(8,128)(2,1)S(1)} copy-done((bf16[1,1,1,12,128,128]{5,4,3,2,1,0:T(8,128)(2,1)S(1)}, bf16[1,1,1,12,128,128]{5,4,3,2,1,0:T(8,128)(2,1)}, u32[]{:S(2)}) %copy-start.4) | copy-done | bytes 393240
  5.6 0.0 copy-start.5
  5.6 1.0 %copy-done.5 = bf16[1,1,1,12,128,128]{5,4,3,2,1,0:T(8,128)(2,1)S(1)} copy-done((bf16[1,1,1,12,128,128]{5,4,3,2,1,0:T(8,128)(2,1)S(1)}, bf16[1,1,1,12,128,128]{5,4,3,2,1,0:T(8,128)(2,1)}, u32[]{:S(2)}) %copy-start.5) | copy-done | bytes 393240
  6.6 0.0 copy-start.6
  6.6 0.9 %copy-done.6 = bf16[1,1,1,12,32,128]{5,4,3,2,1,0:T(8,128)(2,1)S(1)} copy-done((bf16[1,1,1,12,32,128]{5,4,3,2,1,0:T(8,128)(2,1)S(1)}, bf16[1,1,1,12,32,128]{5,4,3,2,1,0:T(8,128)(2,1)}, u32[]{:S(2)}) %copy-start.6) | copy-done | bytes 98328
  7.5 0.0 copy-start.7
  7.5 0.8 %copy-done.7 = bf16[1,1,1,128,128]{4,3,2,1,0:T(8,128)(2,1)S(1)} copy-done((bf16[1,1,1,128,128]{4,3,2,1,0:T(8,128)(2,1)S(1)}, bf16[1,1,1,128,128]{4,3,2,1,0:T(8,128)(2,1)}, u32[]{:S(2)}) %copy-start.7) | copy-done | bytes 32792
  8.3 0.0 copy-start.8
  8.3 0.8 %copy-done.8 = bf16[1,1,1,128,128]{4,3,2,1,0:T(8,128)(2,1)S(1)} copy-done((bf16[1,1,1,128,128]{4,3,2,1,0:T(8,128)(2,1)S(1)}, bf16[1,1,1,128,128]{4,3,2,1,0:T(8,128)(2,1)}, u32[]{:S(2)}) %copy-start.8) | copy-done | bytes 32792
  9.0 0.0 copy-start.9
  9.0 0.8 %copy-done.9 = bf16[1,1,1,128,128]{4,3,2,1,0:T(8,128)(2,1)S(1)} copy-done((bf16[1,1,1,128,128]{4,3,2,1,0:T(8,128)(2,1)S(1)}, bf16[1,1,1,128,128]{4,3,2,1,0:T(8,128)(2,1)}, u32[]{:S(2)}) %copy-start.9) | copy-done | bytes 32792
  9.8 0.0 copy-start.10
  9.8 0.8 %copy-done.10 = bf16[1,1,1,128,128]{4,3,2,1,0:T(8,128)(2,1)S(1)} copy-done((bf16[1,1,1,128,128]{4,3,2,1,0:T(8,128)(2,1)S(1)}, bf16[1,1,1,128,128]{4,3,2,1,0:T(8,128)(2,1)}, u32[]{:S(2)}) %copy-start.10) | copy-done | bytes 32792
  10.5 54.5 %smooth.1 = (bf16[12,32,128]{2,1,0:T(8,128)(2,1)S(1)}, bf16[12,32,128]{2,1,0:T(8,128)(2,1)S(1)}, f32[12,32,128]{2,1,0:T(8,128)S(1)}, f32[32,128]{1,0:T(8,128)S(1)}) custom-call(bf16[12,32,128]{2,1,0:T(8,128)(2,1)S(1)} %bitcast.21, bf16[12,128,128]{2,1,0:T(8,128)(2,1)S(1)} %bitcast.15, bf16[12,128,128]{2,1,0:T(8,128)(2,1)S(1)} %bitcast.16, ...), custom_call_target="tpu_custom_call" | custom-call | tf_op jit(solution)/shard_map/smooth/pallas_call | solution.py:300
  65.1 0.8 %fusion.2 = (f32[1,1,1,12,32,128]{5,4,3,2,1,0:T(8,128)}, f32[1,1,1,12,32,128]{5,4,3,2,1,0:T(8,128)}) fusion(bf16[12,32,128]{2,1,0:T(8,128)(2,1)S(1)} %get-tuple-element.8, f32[12,32,128]{2,1,0:T(8,128)S(1)} %get-tuple-element.9, f32[32,128]{1,0:T(8,128)S(1)} %get-tuple-element.7, bf16[12,32,128]{2,1,0:T(8,128)(2,1)S(1)} %get-tuple-element.6), kind=kLoop, calls=%fused_computation.4 | loop fusion | flops 294912 | bytes 802816 | tf_op jit(solution)/shard_map/reshape | solution.py:347
Async XLA Ops:
  0.6 1.0 %copy-start = (bf16[1,1,1,12,128,128]{5,4,3,2,1,0:T(8,128)(2,1)S(1)}, bf16[1,1,1,12,128,128]{5,4,3,2,1,0:T(8,128)(2,1)}, u32[]{:S(2)}) copy-start(bf16[1,1,1,12,128,128]{5,4,3,2,1,0:T(8,128)(2,1)} %param.12) | copy-start | bytes 1179652
  1.6 1.0 %copy-start.1 = (bf16[1,1,1,12,128,128]{5,4,3,2,1,0:T(8,128)(2,1)S(1)}, bf16[1,1,1,12,128,128]{5,4,3,2,1,0:T(8,128)(2,1)}, u32[]{:S(2)}) copy-start(bf16[1,1,1,12,128,128]{5,4,3,2,1,0:T(8,128)(2,1)} %param.13) | copy-start | bytes 1179652
  2.6 1.0 %copy-start.2 = (bf16[1,1,1,12,128,128]{5,4,3,2,1,0:T(8,128)(2,1)S(1)}, bf16[1,1,1,12,128,128]{5,4,3,2,1,0:T(8,128)(2,1)}, u32[]{:S(2)}) copy-start(bf16[1,1,1,12,128,128]{5,4,3,2,1,0:T(8,128)(2,1)} %param.14) | copy-start | bytes 1179652
  3.6 1.0 %copy-start.3 = (bf16[1,1,1,12,128,128]{5,4,3,2,1,0:T(8,128)(2,1)S(1)}, bf16[1,1,1,12,128,128]{5,4,3,2,1,0:T(8,128)(2,1)}, u32[]{:S(2)}) copy-start(bf16[1,1,1,12,128,128]{5,4,3,2,1,0:T(8,128)(2,1)} %param.15) | copy-start | bytes 1179652
  4.6 1.0 %copy-start.4 = (bf16[1,1,1,12,128,128]{5,4,3,2,1,0:T(8,128)(2,1)S(1)}, bf16[1,1,1,12,128,128]{5,4,3,2,1,0:T(8,128)(2,1)}, u32[]{:S(2)}) copy-start(bf16[1,1,1,12,128,128]{5,4,3,2,1,0:T(8,128)(2,1)} %param.16) | copy-start | bytes 1179652
  5.6 1.0 %copy-start.5 = (bf16[1,1,1,12,128,128]{5,4,3,2,1,0:T(8,128)(2,1)S(1)}, bf16[1,1,1,12,128,128]{5,4,3,2,1,0:T(8,128)(2,1)}, u32[]{:S(2)}) copy-start(bf16[1,1,1,12,128,128]{5,4,3,2,1,0:T(8,128)(2,1)} %param.17) | copy-start | bytes 1179652
  6.6 0.9 %copy-start.6 = (bf16[1,1,1,12,32,128]{5,4,3,2,1,0:T(8,128)(2,1)S(1)}, bf16[1,1,1,12,32,128]{5,4,3,2,1,0:T(8,128)(2,1)}, u32[]{:S(2)}) copy-start(bf16[1,1,1,12,32,128]{5,4,3,2,1,0:T(8,128)(2,1)} %param.11) | copy-start | bytes 294916
  7.5 0.8 %copy-start.7 = (bf16[1,1,1,128,128]{4,3,2,1,0:T(8,128)(2,1)S(1)}, bf16[1,1,1,128,128]{4,3,2,1,0:T(8,128)(2,1)}, u32[]{:S(2)}) copy-start(bf16[1,1,1,128,128]{4,3,2,1,0:T(8,128)(2,1)} %param.18) | copy-start | bytes 98308
  8.3 0.8 %copy-start.8 = (bf16[1,1,1,128,128]{4,3,2,1,0:T(8,128)(2,1)S(1)}, bf16[1,1,1,128,128]{4,3,2,1,0:T(8,128)(2,1)}, u32[]{:S(2)}) copy-start(bf16[1,1,1,128,128]{4,3,2,1,0:T(8,128)(2,1)} %param.19) | copy-start | bytes 98308
  9.0 0.8 %copy-start.9 = (bf16[1,1,1,128,128]{4,3,2,1,0:T(8,128)(2,1)S(1)}, bf16[1,1,1,128,128]{4,3,2,1,0:T(8,128)(2,1)}, u32[]{:S(2)}) copy-start(bf16[1,1,1,128,128]{4,3,2,1,0:T(8,128)(2,1)} %param.20) | copy-start | bytes 98308
  9.8 0.8 %copy-start.10 = (bf16[1,1,1,128,128]{4,3,2,1,0:T(8,128)(2,1)S(1)}, bf16[1,1,1,128,128]{4,3,2,1,0:T(8,128)(2,1)}, u32[]{:S(2)}) copy-start(bf16[1,1,1,128,128]{4,3,2,1,0:T(8,128)(2,1)} %param.21) | copy-start | bytes 98308

commit v2 on v1

--- a/solution.py
+++ b/solution.py
@@ -249,6 +249,7 @@
     sums = jnp.sum(laid, axis=0, keepdims=True)
 
     base = 0
+    sum_copies = []
     for index, phase in enumerate(PHASES):
         sum_out[index] = sums
         copies = []
@@ -265,8 +266,7 @@
             copy.wait_recv()
         for slot in range(len(copies)):
             sums = sums + sum_in[base + slot]
-        for copy in copies:
-            copy.wait_send()
+        sum_copies += copies
         base += len(copies)
 
     wide = jnp.broadcast_to(sums, (RHS, DOF))
@@ -276,7 +276,7 @@
     store_factor = pltpu.make_async_copy(factor, factor_o, store_sem.at[3])
     store_factor.start()
 
-    for copy in coarse_copies:
+    for copy in coarse_copies + sum_copies:
         copy.wait_send()
     for turn in range(2):
         for mu in range(3):
@@ -305,7 +305,7 @@
             jax.ShapeDtypeStruct((NX, RHS, DOF), F32),
             jax.ShapeDtypeStruct((RHS, DOF), F32),
         ),
-        in_specs=[pl.BlockSpec(memory_space=pl.ANY)] * 11,
+        in_specs=[pl.BlockSpec(memory_space=pltpu.HBM)] * 11,
         out_specs=[pl.BlockSpec(memory_space=pl.ANY)] * 4,
         scratch_shapes=[
             vmem((NX, RHS, DOF), BF16),
@@ -337,7 +337,7 @@
             dma((total,)),
         ],
         compiler_params=pltpu.CompilerParams(
-            collective_id=0, has_side_effects=True, vmem_limit_bytes=32 * 1024 * 1024
+            collective_id=0, has_side_effects=True, vmem_limit_bytes=60 * 1024 * 1024
         ),
         name="smooth",
     )(source.reshape(NX, RHS, DOF), *blocks, *tops)

time: 66.5 us -> 56 us (0.84)
  the two profiles are of different devices: /device:TPU:8 before, /device:TPU:1 now
where the time goes in v2:
time: 56 us; the launch traced here: 55 us
  Pallas kernels  52.5 us (94%)
  other arithmetic  1.85 us (3%)
  between operations  0.64 us (1%)
    pallas_call x1, Pallas kernels, body(): pl.pallas_call(kernel, out_shape=(jax.ShapeDtypeStruct((NX, RHS, DOF), BF...  52.5 us
    reshape x1, other arithmetic, body(): return (update.reshape(shape), remainder.reshape(shape))  1.85 us

profile of v2, /device:TPU:1, one launch (start us, length us, event | category | flops | bytes accessed | tf_op | source)
XLA Modules:
  0.0 55.0 jit_solution(236925600498185814)
XLA Ops:
  0.6 52.5 %smooth.1 = (bf16[12,32,128]{2,1,0:T(8,128)(2,1)}, bf16[12,32,128]{2,1,0:T(8,128)(2,1)}, f32[12,32,128]{2,1,0:T(8,128)}, f32[32,128]{1,0:T(8,128)}) custom-call(bf16[12,32,128]{2,1,0:T(8,128)(2,1)} %bitcast.21, bf16[12,128,128]{2,1,0:T(8,128)(2,1)} %bitcast.15, bf16[12,128,128]{2,1,0:T(8,128)(2,1)} %bitcast.16, bf16[12,128,128]{2,1,0:T(8,128)(2,1)} %bitcast.17, ...), custom_call_target="tpu_custom_call" | custom-call | tf_op jit(solution)/shard_map/smooth/pallas_call | solution.py:300
  53.2 1.9 %fusion.2 = (f32[1,1,1,12,32,128]{5,4,3,2,1,0:T(8,128)}, f32[1,1,1,12,32,128]{5,4,3,2,1,0:T(8,128)}) fusion(bf16[12,32,128]{2,1,0:T(8,128)(2,1)} %get-tuple-element.8, f32[12,32,128]{2,1,0:T(8,128)} %get-tuple-element.9, f32[32,128]{1,0:T(8,128)} %get-tuple-element.7, bf16[12,32,128]{2,1,0:T(8,128)(2,1)} %get-tuple-element.6), kind=kLoop, calls=%fused_computation.4 | loop fusion | flops 294912 | bytes 802816 | tf_op jit(solution)/shard_map/reshape | solution.py:347

commit v3 on v2

--- a/solution.py
+++ b/solution.py
@@ -13,9 +13,10 @@
 
 NX, RHS, DOF = 12, 32, 128
 CHUNKS = 2
+LOADS = 4
 SPAN = NX // CHUNKS
 SIZES = {"core": 2, "x": 4, "y": 8, "z": 8}
-PHASES = (("core", "x"), ("y",), ("z",))
+PHASES = (("z",), ("core", "x", "y"))
 
 
 def offsets_of(phase):
@@ -54,6 +55,7 @@
     load_sem, store_sem,
     coarse_send, coarse_recv, field_send, field_recv, back_send, back_recv,
     sum_send, sum_recv,
+    relay_in, relay_send, relay_recv, late_in, met,
 ):
     ta, gz, yx = lax.axis_index("ta"), lax.axis_index("gz"), lax.axis_index("yx")
 
@@ -88,30 +90,62 @@
             place["x"],
         )
 
+    y, z = here["y"], here["z"]
+    low, high = z == 0, z == 7
+    across = partner({"y": 4})
+    below, above = partner({"z": 7}), partner({"z": 1})
+
+    pieces = []
     loads = {}
-    pairs = (
-        ("pro", pro_h, pro),
-        ("src", src_h, src),
-        ("tt", tt_h, tops.at[0]),
-        ("tz", tz_h, tops.at[1]),
-        ("ty", ty_h, tops.at[2]),
-        ("td", td_h, tops.at[3]),
-        ("lt", lt_h, links.at[0]),
-        ("lz", lz_h, links.at[1]),
-        ("ly", ly_h, links.at[2]),
-        ("lx", lx_h, links.at[3]),
-        ("diag", diag_h, diag),
-    )
-    for index, (name, source, target) in enumerate(pairs):
-        loads[name] = pltpu.make_async_copy(source, target, load_sem.at[index])
-        loads[name].start()
+
+    def load(name, source, target):
+        copy = pltpu.make_async_copy(source, target, load_sem.at[len(pieces)])
+        copy.start()
+        pieces.append(name)
+        loads.setdefault(name, []).append(copy)
+
+    def loaded(name):
+        for copy in loads[name]:
+            copy.wait()
+
+    for part in range(LOADS):
+        some = pl.ds(part * (NX // LOADS), NX // LOADS)
+        load(("pro", part), pro_h.at[some], pro.at[some])
+        load(("src", part), src_h.at[some], src.at[some])
+    load("tt", tt_h, tops.at[0])
+    load("tz", tz_h, tops.at[1])
+    load("ty", ty_h, tops.at[2])
+    load("td", td_h, tops.at[3])
+    load("lt", lt_h, links.at[0])
+    load("lz", lz_h, links.at[1])
+    load("ly", ly_h, links.at[2])
+    load("lx", lx_h, links.at[3])
+    load("diag", diag_h, diag)
+
+    def signal(semaphore, device):
+        pl.semaphore_signal(semaphore, inc=1, device_id=device, device_id_type=MESH)
 
     barrier = pltpu.get_barrier_semaphore()
-    greeted = list(plus) + list(minus)
-    for phase in PHASES:
-        greeted += [partner(step) for step in offsets_of(phase)]
-    for device in greeted:
-        pl.semaphore_signal(barrier, inc=1, device_id=device, device_id_type=MESH)
+    for device in [plus[1], minus[1], plus[2], minus[2], partner({"y": 1}), partner({"y": 7})]:
+        signal(barrier, device)
+    for step in offsets_of(("core", "x")):
+        signal(barrier, partner(step))
+
+    @pl.when(low)
+    def _():
+        signal(barrier, minus[0])
+        signal(barrier, below)
+        signal(barrier, across)
+
+    @pl.when(jnp.logical_not(low))
+    def _():
+        signal(barrier, minus[0])
+
+    @pl.when(jnp.logical_not(high))
+    def _():
+        signal(barrier, plus[0])
+
+    greetings = 13 + jnp.where(high, 3, 2)
 
     def remote(source, target, send, recv, device):
         return pltpu.make_async_remote_copy(
@@ -119,35 +153,72 @@
             device_id=device, device_id_type=MESH,
         )
 
-    loads["pro"].wait()
-    loads["src"].wait()
-    restricted = adjoint(src[0], pro[0])
-    for n in range(1, NX):
-        restricted += adjoint(src[n], pro[n])
+    restricted = jnp.zeros((RHS, DOF), F32)
+    for part in range(LOADS):
+        loaded(("pro", part))
+        loaded(("src", part))
+        for n in range(part * (NX // LOADS), (part + 1) * (NX // LOADS)):
+            restricted += adjoint(src[n], pro[n])
     coarse[0] = restricted
     split = halves(restricted)
     for mu, name in enumerate(("tt", "tz", "ty")):
-        loads[name].wait()
+        loaded(name)
         coarse[1 + mu] = fold(adjoint(split, tops[mu]))
 
-    pl.semaphore_wait(barrier, len(greeted))
-
-    coarse_copies = []
-    for mu in range(3):
-        coarse_copies.append(
-            remote(coarse.at[0], coarse_in.at[mu], coarse_send.at[mu], coarse_recv.at[mu], minus[mu])
+    pl.semaphore_wait(barrier, greetings)
+
+    @pl.when(high)
+    def _():
+        signal(late_in, above)
+
+    signal(met.at[0], partner({"y": 1}))
+    signal(met.at[0], partner({"y": 7}))
+
+    @pl.when(jnp.logical_not(low))
+    def _():
+        signal(met.at[0], below)
+
+    @pl.when(jnp.logical_not(jnp.logical_or(low, high)))
+    def _():
+        signal(met.at[0], above)
+
+    def value_copy(mu, device):
+        return remote(coarse.at[0], coarse_in.at[mu], coarse_send.at[mu], coarse_recv.at[mu], device)
+
+    def hop_copy(mu):
+        return remote(
+            coarse.at[1 + mu], hop_in.at[mu], coarse_send.at[3 + mu], coarse_recv.at[3 + mu], plus[mu]
         )
-        coarse_copies.append(
-            remote(coarse.at[1 + mu], hop_in.at[mu], coarse_send.at[3 + mu], coarse_recv.at[3 + mu], plus[mu])
-        )
-    for copy in coarse_copies:
-        copy.start()
-    loads["td"].wait()
+
+    hop_copy(0).start()
+    to_relay = remote(coarse.at[0], relay_in, relay_send.at[0], relay_recv, across)
+    from_relay = remote(relay_in, coarse_in.at[0], relay_send.at[1], coarse_recv.at[0], below)
+
+    @pl.when(low)
+    def _():
+        to_relay.start()
+
+    @pl.when(jnp.logical_not(low))
+    def _():
+        value_copy(0, minus[0]).start()
+
+    for mu in (1, 2):
+        value_copy(mu, minus[mu]).start()
+        hop_copy(mu).start()
+
+    @pl.when(low)
+    def _():
+        to_relay.wait_recv()
+        pl.semaphore_wait(late_in, 1)
+        from_relay.start()
+        signal(met.at[0], above)
+
+    loaded("td")
     correction = fold(forward(split, tops[3]))
     for mu in (2, 1, 0):
-        coarse_copies[2 * mu].wait_recv()
+        value_copy(mu, minus[mu]).wait_recv()
         correction += fold(forward(halves(coarse_in[mu]), tops[mu]))
-        coarse_copies[2 * mu + 1].wait_recv()
+        hop_copy(mu).wait_recv()
         correction += hop_in[mu]
     coarse_fix = correction.astype(BF16)
 
@@ -205,13 +276,16 @@
             field[0, n] = forward(coarse_fix, pro[n]).astype(BF16)
         send_field(0, part)
     for mu, name in enumerate(("lt", "lz", "ly")):
-        loads[name].wait()
+        loaded(name)
         for part in range(CHUNKS):
             send_back(0, mu, part)
+    pl.semaphore_wait(met.at[0], 2 + jnp.where(jnp.logical_or(low, high), 1, 2))
+    for step in ({"y": 2}, {"y": 6}, {"z": 2}, {"z": 6}):
+        signal(met.at[1], partner(step))
     store_lifted = pltpu.make_async_copy(field.at[0], lifted_o, store_sem.at[0])
     store_lifted.start()
-    loads["lx"].wait()
-    loads["diag"].wait()
+    loaded("lx")
+    loaded("diag")
     local_terms(0)
     near_terms(0)
     for part in range(CHUNKS):
@@ -227,6 +301,9 @@
     store_resid = pltpu.make_async_copy(field.at[1], resid_o, store_sem.at[1])
     store_resid.start()
 
+    pl.semaphore_wait(met.at[1], 4)
+    signal(met.at[2], across)
+
     local_terms(1)
     near_terms(1)
     cross = jnp.zeros((RHS, DOF), F32)
@@ -248,6 +325,7 @@
     laid = jnp.where(lane == row, cross_at, jnp.where(lane == row + RHS, energy_at, 0.0))
     sums = jnp.sum(laid, axis=0, keepdims=True)
 
+    pl.semaphore_wait(met.at[2], 1)
     base = 0
     sum_copies = []
     for index, phase in enumerate(PHASES):
@@ -276,7 +354,20 @@
     store_factor = pltpu.make_async_copy(factor, factor_o, store_sem.at[3])
     store_factor.start()
 
-    for copy in coarse_copies + sum_copies:
+    @pl.when(low)
+    def _():
+        to_relay.wait_send()
+        from_relay.wait_send()
+
+    @pl.when(jnp.logical_not(low))
+    def _():
+        value_copy(0, minus[0]).wait_send()
+
+    for mu in range(3):
+        if mu:
+            value_copy(mu, minus[mu]).wait_send()
+        hop_copy(mu).wait_send()
+    for copy in sum_copies:
         copy.wait_send()
     for turn in range(2):
         for mu in range(3):
@@ -325,7 +416,7 @@
             vmem((3, RHS, DOF), F32),
             vmem((len(PHASES), 1, DOF), F32),
             vmem((total, 1, DOF), F32),
-            dma((11,)),
+            dma((2 * LOADS + 9,)),
             dma((4,)),
             dma((6,)),
             dma((6,)),
@@ -335,6 +426,11 @@
             dma((2, 3, CHUNKS)),
             dma((total,)),
             dma((total,)),
+            vmem((RHS, DOF), F32),
+            dma((2,)),
+            dma,
+            pltpu.SemaphoreType.REGULAR,
+            pltpu.SemaphoreType.REGULAR((3,)),
         ],
         compiler_params=pltpu.CompilerParams(
             collective_id=0, has_side_effects=True, vmem_limit_bytes=60 * 1024 * 1024

time: 56 us -> 53.9 us (0.963); the launches traced: 55 us -> 53.8 us
  Pallas kernels: 52.5 us -> 51.3 us
    pallas_call x1, Pallas kernels: 52.5 us -> 51.3 us  [body(): pl.pallas_call(kernel, out_shape=(jax.ShapeDtypeStruct((NX, RHS, DOF), BF...]
where the time goes in v3:
time: 53.9 us; the launch traced here: 53.8 us
  Pallas kernels  51.3 us (95%)
  other arithmetic  1.85 us (3%)
  between operations  0.64 us (1%)
    pallas_call x1, Pallas kernels, body(): pl.pallas_call(kernel, out_shape=(jax.ShapeDtypeStruct((NX, RHS, DOF), BF...  51.3 us
    reshape x1, other arithmetic, body(): return (update.reshape(shape), remainder.reshape(shape))  1.85 us

profile of v3, /device:TPU:1, one launch (start us, length us, event | category | flops | bytes accessed | tf_op | source)
XLA Modules:
  0.0 53.8 jit_solution(10614641954722084390)
XLA Ops:
  0.6 51.3 %smooth.1 = (bf16[12,32,128]{2,1,0:T(8,128)(2,1)}, bf16[12,32,128]{2,1,0:T(8,128)(2,1)}, f32[12,32,128]{2,1,0:T(8,128)}, f32[32,128]{1,0:T(8,128)}) custom-call(bf16[12,32,128]{2,1,0:T(8,128)(2,1)} %bitcast.21, bf16[12,128,128]{2,1,0:T(8,128)(2,1)} %bitcast.15, bf16[12,128,128]{2,1,0:T(8,128)(2,1)} %bitcast.16, bf16[12,128,128]{2,1,0:T(8,128)(2,1)} %bitcast.17, ...), custom_call_target="tpu_custom_call" | custom-call | tf_op jit(solution)/shard_map/smooth/pallas_call | solution.py:391
  51.9 1.9 %fusion.2 = (f32[1,1,1,12,32,128]{5,4,3,2,1,0:T(8,128)}, f32[1,1,1,12,32,128]{5,4,3,2,1,0:T(8,128)}) fusion(bf16[12,32,128]{2,1,0:T(8,128)(2,1)} %get-tuple-element.8, f32[12,32,128]{2,1,0:T(8,128)} %get-tuple-element.9, f32[32,128]{1,0:T(8,128)} %get-tuple-element.7, bf16[12,32,128]{2,1,0:T(8,128)(2,1)} %get-tuple-element.6), kind=kLoop, calls=%fused_computation.4 | loop fusion | flops 294912 | bytes 802816 | tf_op jit(solution)/shard_map/reshape | solution.py:443

commit v4 on v3

--- a/solution.py
+++ b/solution.py
@@ -47,12 +47,12 @@
 
 def kernel(
     src_h, diag_h, lt_h, lz_h, ly_h, lx_h, pro_h, td_h, tt_h, tz_h, ty_h,
-    lifted_o, resid_o, image_o, factor_o,
+    field, image, factor,
     src, diag, links, pro, tops,
-    field, back, field_in, back_in, total, image, factor,
+    back, field_in, back_in, total,
     coarse, coarse_in, hop_in,
     sum_out, sum_in,
-    load_sem, store_sem,
+    load_sem,
     coarse_send, coarse_recv, field_send, field_recv, back_send, back_recv,
     sum_send, sum_recv,
     relay_in, relay_send, relay_recv, late_in, met,
@@ -240,10 +240,6 @@
     def sites(part):
         return range(part * SPAN, (part + 1) * SPAN)
 
-    def send_field(turn, part):
-        for mu in range(3):
-            field_copy(turn, mu, part).start()
-
     def send_back(turn, mu, part):
         for n in sites(part):
             back[turn, mu, n] = adjoint(field[turn, n], links[mu, n]).astype(BF16)
@@ -271,19 +267,26 @@
                 for n in sites(part):
                     total[n] += hop_terms(turn, mu, n)
 
+    def send_near(turn):
+        for mu in (1, 2):
+            for part in range(CHUNKS):
+                field_copy(turn, mu, part).start()
+        for mu in (1, 2):
+            for part in range(CHUNKS):
+                send_back(turn, mu, part)
+
+    loaded("lt")
     for part in range(CHUNKS):
         for n in sites(part):
             field[0, n] = forward(coarse_fix, pro[n]).astype(BF16)
-        send_field(0, part)
-    for mu, name in enumerate(("lt", "lz", "ly")):
-        loaded(name)
-        for part in range(CHUNKS):
-            send_back(0, mu, part)
+        field_copy(0, 0, part).start()
+        send_back(0, 0, part)
+    loaded("lz")
+    loaded("ly")
+    send_near(0)
     pl.semaphore_wait(met.at[0], 2 + jnp.where(jnp.logical_or(low, high), 1, 2))
     for step in ({"y": 2}, {"y": 6}, {"z": 2}, {"z": 6}):
         signal(met.at[1], partner(step))
-    store_lifted = pltpu.make_async_copy(field.at[0], lifted_o, store_sem.at[0])
-    store_lifted.start()
     loaded("lx")
     loaded("diag")
     local_terms(0)
@@ -293,13 +296,9 @@
         for n in sites(part):
             applied = total[n] + hop_terms(0, 0, n)
             field[1, n] = (src[n].astype(F32) - applied).astype(BF16)
-        send_field(1, part)
+        field_copy(1, 0, part).start()
         send_back(1, 0, part)
-    for mu in (1, 2):
-        for part in range(CHUNKS):
-            send_back(1, mu, part)
-    store_resid = pltpu.make_async_copy(field.at[1], resid_o, store_sem.at[1])
-    store_resid.start()
+    send_near(1)
 
     pl.semaphore_wait(met.at[1], 4)
     signal(met.at[2], across)
@@ -315,8 +314,6 @@
             image[n] = value
             cross += value * field[1, n].astype(F32)
             energy += value * value
-    store_image = pltpu.make_async_copy(image, image_o, store_sem.at[2])
-    store_image.start()
 
     row = lax.broadcasted_iota(jnp.int32, (RHS, DOF), 0)
     lane = lax.broadcasted_iota(jnp.int32, (RHS, DOF), 1)
@@ -351,8 +348,6 @@
     cross_sum = jnp.sum(jnp.where(lane == row, wide, 0.0), axis=1, keepdims=True)
     energy_sum = jnp.sum(jnp.where(lane == row + RHS, wide, 0.0), axis=1, keepdims=True)
     factor[...] = jnp.broadcast_to(cross_sum / (energy_sum + 1e-06), (RHS, DOF))
-    store_factor = pltpu.make_async_copy(factor, factor_o, store_sem.at[3])
-    store_factor.start()
 
     @pl.when(low)
     def _():
@@ -374,8 +369,6 @@
             for part in range(CHUNKS):
                 field_copy(turn, mu, part).wait_send()
                 back_copy(turn, mu, part).wait_send()
-    for copy in (store_lifted, store_resid, store_image, store_factor):
-        copy.wait()
 
 
 def body(source, diag_block, link_time, link_zaxis, link_yaxis, link_xaxis, prolong,
@@ -388,36 +381,31 @@
     tops = [value.reshape(DOF, DOF) for value in (top_diag, top_time, top_zaxis, top_yaxis)]
     vmem, dma = pltpu.VMEM, pltpu.SemaphoreType.DMA
     total = sum(COUNTS)
-    lifted, resid, image, factor = pl.pallas_call(
+    field, image, factor = pl.pallas_call(
         kernel,
         out_shape=(
-            jax.ShapeDtypeStruct((NX, RHS, DOF), BF16),
-            jax.ShapeDtypeStruct((NX, RHS, DOF), BF16),
-            jax.ShapeDtypeStruct((NX, RHS, DOF), F32),
-            jax.ShapeDtypeStruct((RHS, DOF), F32),
+            vmem((2, NX, RHS, DOF), BF16),
+            vmem((NX, RHS, DOF), F32),
+            vmem((RHS, DOF), F32),
         ),
         in_specs=[pl.BlockSpec(memory_space=pltpu.HBM)] * 11,
-        out_specs=[pl.BlockSpec(memory_space=pl.ANY)] * 4,
+        out_specs=[pl.BlockSpec(memory_space=pltpu.VMEM)] * 3,
         scratch_shapes=[
             vmem((NX, RHS, DOF), BF16),
             vmem((NX, DOF, DOF), BF16),
             vmem((4, NX, DOF, DOF), BF16),
             vmem((NX, DOF, DOF), BF16),
             vmem((4, DOF, DOF), BF16),
-            vmem((2, NX, RHS, DOF), BF16),
             vmem((2, 3, NX, RHS, DOF), BF16),
             vmem((2, 3, NX, RHS, DOF), BF16),
             vmem((2, 3, NX, RHS, DOF), BF16),
             vmem((NX, RHS, DOF), F32),
-            vmem((NX, RHS, DOF), F32),
-            vmem((RHS, DOF), F32),
             vmem((4, RHS, DOF), F32),
             vmem((3, RHS, DOF), F32),
             vmem((3, RHS, DOF), F32),
             vmem((len(PHASES), 1, DOF), F32),
             vmem((total, 1, DOF), F32),
             dma((2 * LOADS + 9,)),
-            dma((4,)),
             dma((6,)),
             dma((6,)),
             dma((2, 3, CHUNKS)),
@@ -437,8 +425,8 @@
         ),
         name="smooth",
     )(source.reshape(NX, RHS, DOF), *blocks, *tops)
-    wide = resid.astype(F32)
-    update = lifted.astype(F32) + factor * wide
+    wide = field[1].astype(F32)
+    update = field[0].astype(F32) + factor * wide
     remainder = wide - factor * image
     return update.reshape(shape), remainder.reshape(shape)
 

time: 53.9 us -> 51.9 us (0.963)
  Pallas kernels: 51.3 us -> 49.7 us
    pallas_call x1, Pallas kernels: 51.3 us -> 49.7 us  [body(): pl.pallas_call(kernel, out_shape=(vmem((2, NX, RHS, DOF), BF16), vmem((NX...]
    reshape x1, other arithmetic: 1.85 us -> 0.7 us  [body(): return (update.reshape(shape), remainder.reshape(shape))]
    add x0 -> x1, other arithmetic: none -> 0.7 us  [body(): update = field[0].astype(F32) + factor * wide]
where the time goes in v4:
time: 51.9 us; the launch traced here: 51.8 us
  Pallas kernels  49.7 us (96%)
  other arithmetic  1.41 us (3%)
  between operations  0.64 us (1%)
    pallas_call x1, Pallas kernels, body(): pl.pallas_call(kernel, out_shape=(vmem((2, NX, RHS, DOF), BF16), vmem((NX...  49.7 us

profile of v4, /device:TPU:1, one launch (start us, length us, event | category | flops | bytes accessed | tf_op | source)
XLA Modules:
  0.0 51.8 jit_solution(12192756639225208057)
XLA Ops:
  0.6 49.7 %smooth.1 = (bf16[2,12,32,128]{3,2,1,0:T(8,128)(2,1)S(1)}, f32[12,32,128]{2,1,0:T(8,128)S(1)}, f32[32,128]{1,0:T(8,128)S(1)}) custom-call(bf16[12,32,128]{2,1,0:T(8,128)(2,1)} %bitcast.34, bf16[12,128,128]{2,1,0:T(8,128)(2,1)} %bitcast.28, bf16[12,128,128]{2,1,0:T(8,128)(2,1)} %bitcast.29, bf16[12,128,128]{2,1,0:T(8,128)(2,1)} %bitcast.30, ...), custom_call_target="tpu_custom_call" | custom-call | tf_op jit(solution)/shard_map/smooth/pallas_call | solution.py:384
  50.4 0.7 %fusion.3 = f32[1,1,1,12,32,128]{5,4,3,2,1,0:T(8,128)} fusion(f32[12,32,128]{2,1,0:T(8,128)S(1)} %get-tuple-element.7, f32[32,128]{1,0:T(8,128)S(1)} %get-tuple-element.6, bf16[2,12,32,128]{3,2,1,0:T(8,128)(2,1)S(1)} %get-tuple-element.5), kind=kLoop, calls=%fused_computation.5 | loop fusion | flops 147456 | bytes 507904 | tf_op jit(solution)/shard_map/reshape | solution.py:431
  51.1 0.7 %fusion.1 = f32[1,1,1,12,32,128]{5,4,3,2,1,0:T(8,128)} fusion(f32[32,128]{1,0:T(8,128)S(1)} %get-tuple-element.6, bf16[2,12,32,128]{3,2,1,0:T(8,128)(2,1)S(1)} %get-tuple-element.5), kind=kLoop, calls=%fused_computation.3 | loop fusion | flops 196608 | bytes 409600 | tf_op jit(solution)/shard_map/add | solution.py:429

commit v5 on v4

--- a/solution.py
+++ b/solution.py
@@ -16,15 +16,15 @@
 LOADS = 4
 SPAN = NX // CHUNKS
 SIZES = {"core": 2, "x": 4, "y": 8, "z": 8}
-PHASES = (("z",), ("core", "x", "y"))
-
-
-def offsets_of(phase):
-    every = itertools.product(*(range(SIZES[axis]) for axis in phase))
-    return [dict(zip(phase, step)) for step in every if any(step)]
-
-
-COUNTS = [len(offsets_of(phase)) for phase in PHASES]
+EARLY = 4
+
+
+def offsets_of(axes):
+    every = itertools.product(*(range(SIZES[axis]) for axis in axes))
+    return [dict(zip(axes, step)) for step in every if any(step)]
+
+
+PLANE = [{}] + offsets_of(("core", "x"))
 
 
 def forward(vector, block):
@@ -47,16 +47,18 @@
 
 def kernel(
     src_h, diag_h, lt_h, lz_h, ly_h, lx_h, pro_h, td_h, tt_h, tz_h, ty_h,
-    field, image, factor,
+    lifted, resid, image, factor,
     src, diag, links, pro, tops,
     back, field_in, back_in, total,
     coarse, coarse_in, hop_in,
-    sum_out, sum_in,
+    sum_out, sum_in, direct_in,
     load_sem,
     coarse_send, coarse_recv, field_send, field_recv, back_send, back_recv,
     sum_send, sum_recv,
+    direct_send, direct_recv,
     relay_in, relay_send, relay_recv, late_in, met,
 ):
+    field = (lifted, resid)
     ta, gz, yx = lax.axis_index("ta"), lax.axis_index("gz"), lax.axis_index("yx")
 
     def at(ta_at, gz_at, yx_at):
@@ -81,7 +83,7 @@
 
     def partner(step):
         place = {
-            axis: lax.rem(here[axis] + step.get(axis, 0), size) if step.get(axis, 0) else here[axis]
+            axis: lax.rem(here[axis] + step[axis], size) if axis in step else here[axis]
             for axis, size in SIZES.items()
         }
         return at(
@@ -94,6 +96,14 @@
     low, high = z == 0, z == 7
     across = partner({"y": 4})
     below, above = partner({"z": 7}), partner({"z": 1})
+
+    direct_in[...] = jnp.zeros_like(direct_in)
+    for slot in range(EARLY):
+        sum_in[slot] = jnp.zeros((1, DOF), F32)
+
+    def partner_at(depth, step):
+        ta_at, gz_at, yx_at = partner(step)
+        return at((ta_at // 8) * 8 + depth, gz_at, yx_at)
 
     pieces = []
     loads = {}
@@ -227,7 +237,7 @@
 
     def field_copy(turn, mu, part):
         return remote(
-            field.at[turn, span(part)], field_in.at[turn, mu, span(part)],
+            field[turn].at[span(part)], field_in.at[turn, mu, span(part)],
             field_send.at[turn, mu, part], field_recv.at[turn, mu, part], minus[mu],
         )
 
@@ -242,15 +252,15 @@
 
     def send_back(turn, mu, part):
         for n in sites(part):
-            back[turn, mu, n] = adjoint(field[turn, n], links[mu, n]).astype(BF16)
+            back[turn, mu, n] = adjoint(field[turn][n], links[mu, n]).astype(BF16)
         back_copy(turn, mu, part).start()
 
     def local_terms(turn):
         for n in range(NX):
             after, before = (n + 1) % NX, (n - 1) % NX
-            value = forward(field[turn, n], diag[n])
-            value += forward(field[turn, after], links[3, n])
-            value += adjoint(field[turn, before], links[3, before]).astype(BF16).astype(F32)
+            value = forward(field[turn][n], diag[n])
+            value += forward(field[turn][after], links[3, n])
+            value += adjoint(field[turn][before], links[3, before]).astype(BF16).astype(F32)
             total[n] = value
 
     def arrived(turn, mu, part):
@@ -278,7 +288,7 @@
     loaded("lt")
     for part in range(CHUNKS):
         for n in sites(part):
-            field[0, n] = forward(coarse_fix, pro[n]).astype(BF16)
+            field[0][n] = forward(coarse_fix, pro[n]).astype(BF16)
         field_copy(0, 0, part).start()
         send_back(0, 0, part)
     loaded("lz")
@@ -291,19 +301,24 @@
     loaded("diag")
     local_terms(0)
     near_terms(0)
+    pl.semaphore_wait(met.at[1], 4)
+    signal(met.at[2], across)
     for part in range(CHUNKS):
         arrived(0, 0, part)
         for n in sites(part):
             applied = total[n] + hop_terms(0, 0, n)
-            field[1, n] = (src[n].astype(F32) - applied).astype(BF16)
+            field[1][n] = (src[n].astype(F32) - applied).astype(BF16)
         field_copy(1, 0, part).start()
         send_back(1, 0, part)
     send_near(1)
 
-    pl.semaphore_wait(met.at[1], 4)
-    signal(met.at[2], across)
-
     local_terms(1)
+    pl.semaphore_wait(met.at[2], 1)
+
+    @pl.when(z < EARLY)
+    def _():
+        signal(met.at[3], partner_at(7, {}))
+
     near_terms(1)
     cross = jnp.zeros((RHS, DOF), F32)
     energy = jnp.zeros((RHS, DOF), F32)
@@ -312,7 +327,7 @@
         for n in sites(part):
             value = total[n] + hop_terms(1, 0, n)
             image[n] = value
-            cross += value * field[1, n].astype(F32)
+            cross += value * field[1][n].astype(F32)
             energy += value * value
 
     row = lax.broadcasted_iota(jnp.int32, (RHS, DOF), 0)
@@ -322,27 +337,61 @@
     laid = jnp.where(lane == row, cross_at, jnp.where(lane == row + RHS, energy_at, 0.0))
     sums = jnp.sum(laid, axis=0, keepdims=True)
 
-    pl.semaphore_wait(met.at[2], 1)
-    base = 0
-    sum_copies = []
-    for index, phase in enumerate(PHASES):
-        sum_out[index] = sums
-        copies = []
-        for slot, step in enumerate(offsets_of(phase)):
-            copies.append(
-                remote(
-                    sum_out.at[index], sum_in.at[base + slot],
-                    sum_send.at[base + slot], sum_recv.at[base + slot], partner(step),
-                )
-            )
-        for copy in copies:
-            copy.start()
-        for copy in copies:
-            copy.wait_recv()
-        for slot in range(len(copies)):
-            sums = sums + sum_in[base + slot]
-        sum_copies += copies
-        base += len(copies)
+    own = sum_out.at[0]
+    sum_out[0] = sums
+
+    def own_copy(slot, depth, step):
+        return remote(
+            own, direct_in.at[slot], direct_send.at[depth], direct_recv, partner_at(depth, step)
+        )
+
+    @pl.when(high)
+    def _():
+        pl.semaphore_wait(met.at[3], EARLY)
+        for depth in range(EARLY):
+
+            def spread(turned, carry):
+                along = lax.rem(turned + 4, 8)
+                for slot, step in enumerate(PLANE):
+                    own_copy(along * len(PLANE) + slot, depth, {**step, "y": along}).start()
+                return carry
+
+            lax.fori_loop(0, 8, spread, 0)
+
+    def along_copy(slot):
+        return remote(
+            own, sum_in.at[slot], sum_send.at[slot], sum_recv.at[slot], partner({"z": slot + 1})
+        )
+
+    def some(slot, hidden, act):
+        if slot < EARLY:
+            pl.when(jnp.logical_not(hidden))(act)
+        else:
+            act()
+
+    for slot in range(7):
+        some(slot, high, lambda: along_copy(slot).start())
+    for slot in range(7):
+        some(slot, z == slot, lambda: along_copy(slot).wait_recv())
+    for slot in range(7):
+        sums = sums + sum_in[slot]
+
+    sum_out[1] = sums
+    plane_copies = [
+        remote(sum_out.at[1], sum_in.at[7 + slot], sum_send.at[7 + slot], sum_recv.at[7 + slot], partner(step))
+        for slot, step in enumerate(offsets_of(("core", "x", "y")))
+    ]
+    for copy in plane_copies:
+        copy.start()
+    for copy in plane_copies:
+        copy.wait_recv()
+    sums = sums + jnp.sum(sum_in[7:], axis=0)
+
+    @pl.when(z < EARLY)
+    def _():
+        pltpu.make_async_copy(direct_in, direct_in, direct_recv).wait()
+
+    sums = sums + jnp.sum(direct_in[...], axis=0)
 
     wide = jnp.broadcast_to(sums, (RHS, DOF))
     cross_sum = jnp.sum(jnp.where(lane == row, wide, 0.0), axis=1, keepdims=True)
@@ -362,8 +411,16 @@
         if mu:
             value_copy(mu, minus[mu]).wait_send()
         hop_copy(mu).wait_send()
-    for copy in sum_copies:
+    for slot in range(7):
+        some(slot, high, lambda: along_copy(slot).wait_send())
+    for copy in plane_copies:
         copy.wait_send()
+
+    @pl.when(high)
+    def _():
+        for depth in range(EARLY):
+            pltpu.make_async_copy(direct_in, direct_in, direct_send.at[depth]).wait()
+
     for turn in range(2):
         for mu in range(3):
             for part in range(CHUNKS):
@@ -380,16 +437,17 @@
     ]
     tops = [value.reshape(DOF, DOF) for value in (top_diag, top_time, top_zaxis, top_yaxis)]
     vmem, dma = pltpu.VMEM, pltpu.SemaphoreType.DMA
-    total = sum(COUNTS)
-    field, image, factor = pl.pallas_call(
+    total = 7 + 63
+    lifted, resid, image, factor = pl.pallas_call(
         kernel,
         out_shape=(
-            vmem((2, NX, RHS, DOF), BF16),
+            vmem((NX, RHS, DOF), BF16),
+            vmem((NX, RHS, DOF), BF16),
             vmem((NX, RHS, DOF), F32),
             vmem((RHS, DOF), F32),
         ),
         in_specs=[pl.BlockSpec(memory_space=pltpu.HBM)] * 11,
-        out_specs=[pl.BlockSpec(memory_space=pltpu.VMEM)] * 3,
+        out_specs=[pl.BlockSpec(memory_space=pltpu.VMEM)] * 4,
         scratch_shapes=[
             vmem((NX, RHS, DOF), BF16),
             vmem((NX, DOF, DOF), BF16),
@@ -403,8 +461,9 @@
             vmem((4, RHS, DOF), F32),
             vmem((3, RHS, DOF), F32),
             vmem((3, RHS, DOF), F32),
-            vmem((len(PHASES), 1, DOF), F32),
+            vmem((2, 1, DOF), F32),
             vmem((total, 1, DOF), F32),
+            vmem((64, 1, DOF), F32),
             dma((2 * LOADS + 9,)),
             dma((6,)),
             dma((6,)),
@@ -414,19 +473,21 @@
             dma((2, 3, CHUNKS)),
             dma((total,)),
             dma((total,)),
+            dma((EARLY,)),
+            dma,
             vmem((RHS, DOF), F32),
             dma((2,)),
             dma,
             pltpu.SemaphoreType.REGULAR,
-            pltpu.SemaphoreType.REGULAR((3,)),
+            pltpu.SemaphoreType.REGULAR((4,)),
         ],
         compiler_params=pltpu.CompilerParams(
             collective_id=0, has_side_effects=True, vmem_limit_bytes=60 * 1024 * 1024
         ),
         name="smooth",
     )(source.reshape(NX, RHS, DOF), *blocks, *tops)
-    wide = field[1].astype(F32)
-    update = field[0].astype(F32) + factor * wide
+    wide = resid.astype(F32)
+    update = lifted.astype(F32) + factor * wide
     remainder = wide - factor * image
     return update.reshape(shape), remainder.reshape(shape)
 

time: 51.9 us -> 49.3 us (0.950)
  Pallas kernels: 49.7 us -> 47.7 us
  other arithmetic: 1.41 us -> 0.79 us
    pallas_call x1, Pallas kernels: 49.7 us -> 47.7 us  [body(): pl.pallas_call(kernel, out_shape=(vmem((NX, RHS, DOF), BF16), vmem((NX, R...]
    add x1 -> x0, other arithmetic: 0.7 us -> none  [body(): update = field[0].astype(F32) + factor * wide]
where the time goes in v5:
time: 49.3 us; the launch traced here: 49.1 us
  Pallas kernels  47.7 us (97%)
  other arithmetic  0.79 us (2%)
  between operations  0.64 us (1%)
    pallas_call x1, Pallas kernels, body(): pl.pallas_call(kernel, out_shape=(vmem((NX, RHS, DOF), BF16), vmem((NX, R...  47.7 us

profile of v5, /device:TPU:1, one launch (start us, length us, event | category | flops | bytes accessed | tf_op | source)
XLA Modules:
  0.0 49.1 jit_solution(9714124359200625040)
XLA Ops:
  0.6 47.7 %smooth.1 = (bf16[12,32,128]{2,1,0:T(8,128)(2,1)S(1)}, bf16[12,32,128]{2,1,0:T(8,128)(2,1)S(1)}, f32[12,32,128]{2,1,0:T(8,128)S(1)}, f32[32,128]{1,0:T(8,128)S(1)}) custom-call(bf16[12,32,128]{2,1,0:T(8,128)(2,1)} %bitcast.21, bf16[12,128,128]{2,1,0:T(8,128)(2,1)} %bitcast.15, bf16[12,128,128]{2,1,0:T(8,128)(2,1)} %bitcast.16, ...), custom_call_target="tpu_custom_call" | custom-call | tf_op jit(solution)/shard_map/smooth/pallas_call | solution.py:441
  48.3 0.8 %fusion.2 = (f32[1,1,1,12,32,128]{5,4,3,2,1,0:T(8,128)}, f32[1,1,1,12,32,128]{5,4,3,2,1,0:T(8,128)}) fusion(bf16[12,32,128]{2,1,0:T(8,128)(2,1)S(1)} %get-tuple-element.8, f32[12,32,128]{2,1,0:T(8,128)S(1)} %get-tuple-element.9, f32[32,128]{1,0:T(8,128)S(1)} %get-tuple-element.7, bf16[12,32,128]{2,1,0:T(8,128)(2,1)S(1)} %get-tuple-element.6), kind=kLoop, calls=%fused_computation.4 | loop fusion | flops 294912 | bytes 802816 | tf_op jit(solution)/shard_map/reshape | solution.py:492

commit v6 on v5

--- a/solution.py
+++ b/solution.py
@@ -13,7 +13,7 @@
 
 NX, RHS, DOF = 12, 32, 128
 CHUNKS = 2
-LOADS = 4
+LOADS = 2
 SPAN = NX // CHUNKS
 SIZES = {"core": 2, "x": 4, "y": 8, "z": 8}
 EARLY = 4
@@ -52,11 +52,9 @@
     back, field_in, back_in, total,
     coarse, coarse_in, hop_in,
     sum_out, sum_in, direct_in,
-    load_sem,
-    coarse_send, coarse_recv, field_send, field_recv, back_send, back_recv,
-    sum_send, sum_recv,
-    direct_send, direct_recv,
-    relay_in, relay_send, relay_recv, late_in, met,
+    load_sem, coarse_send, coarse_recv, field_send, near_recv, wrap_recv,
+    sum_send, sum_recv, direct_send, direct_recv,
+    relay_in, relay_recv, late_in, met,
 ):
     field = (lifted, resid)
     ta, gz, yx = lax.axis_index("ta"), lax.axis_index("gz"), lax.axis_index("yx")
@@ -105,32 +103,21 @@
         ta_at, gz_at, yx_at = partner(step)
         return at((ta_at // 8) * 8 + depth, gz_at, yx_at)
 
-    pieces = []
-    loads = {}
-
-    def load(name, source, target):
-        copy = pltpu.make_async_copy(source, target, load_sem.at[len(pieces)])
-        copy.start()
-        pieces.append(name)
-        loads.setdefault(name, []).append(copy)
-
-    def loaded(name):
-        for copy in loads[name]:
-            copy.wait()
+    def taken(ref, semaphore):
+        pltpu.make_async_copy(ref, ref, semaphore).wait()
+
+    def load(source, target, slot):
+        pltpu.make_async_copy(source, target, load_sem.at[slot]).start()
 
     for part in range(LOADS):
         some = pl.ds(part * (NX // LOADS), NX // LOADS)
-        load(("pro", part), pro_h.at[some], pro.at[some])
-        load(("src", part), src_h.at[some], src.at[some])
-    load("tt", tt_h, tops.at[0])
-    load("tz", tz_h, tops.at[1])
-    load("ty", ty_h, tops.at[2])
-    load("td", td_h, tops.at[3])
-    load("lt", lt_h, links.at[0])
-    load("lz", lz_h, links.at[1])
-    load("ly", ly_h, links.at[2])
-    load("lx", lx_h, links.at[3])
-    load("diag", diag_h, diag)
+        load(pro_h.at[some], pro.at[some], 2 * part)
+        load(src_h.at[some], src.at[some], 2 * part + 1)
+    for slot, source in enumerate((tt_h, tz_h, ty_h, td_h)):
+        load(source, tops.at[slot], 2 * LOADS)
+    for slot, source in enumerate((lt_h, lz_h, ly_h, lx_h)):
+        load(source, links.at[slot], 2 * LOADS + 1)
+    load(diag_h, diag, 2 * LOADS + 2)
 
     def signal(semaphore, device):
         pl.semaphore_signal(semaphore, inc=1, device_id=device, device_id_type=MESH)
@@ -165,17 +152,38 @@
 
     restricted = jnp.zeros((RHS, DOF), F32)
     for part in range(LOADS):
-        loaded(("pro", part))
-        loaded(("src", part))
+        some = pl.ds(part * (NX // LOADS), NX // LOADS)
+        taken(pro.at[some], load_sem.at[2 * part])
+        taken(src.at[some], load_sem.at[2 * part + 1])
         for n in range(part * (NX // LOADS), (part + 1) * (NX // LOADS)):
             restricted += adjoint(src[n], pro[n])
     coarse[0] = restricted
     split = halves(restricted)
-    for mu, name in enumerate(("tt", "tz", "ty")):
-        loaded(name)
-        coarse[1 + mu] = fold(adjoint(split, tops[mu]))
+    taken(tops, load_sem.at[2 * LOADS])
+    coarse[1] = fold(adjoint(split, tops[0]))
 
     pl.semaphore_wait(barrier, greetings)
+
+    def value_copy(mu, device):
+        return remote(coarse.at[0], coarse_in.at[mu], coarse_send, coarse_recv.at[min(mu, 1)], device)
+
+    def hop_copy(mu):
+        return remote(coarse.at[1 + mu], hop_in.at[mu], coarse_send, coarse_recv.at[min(mu, 1)], plus[mu])
+
+    hop_copy(0).start()
+    to_relay = remote(coarse.at[0], relay_in, coarse_send, relay_recv, across)
+    from_relay = remote(relay_in, coarse_in.at[0], coarse_send, coarse_recv.at[0], below)
+
+    @pl.when(low)
+    def _():
+        to_relay.start()
+
+    @pl.when(jnp.logical_not(low))
+    def _():
+        value_copy(0, minus[0]).start()
+
+    for mu in (1, 2):
+        value_copy(mu, minus[mu]).start()
 
     @pl.when(high)
     def _():
@@ -192,28 +200,8 @@
     def _():
         signal(met.at[0], above)
 
-    def value_copy(mu, device):
-        return remote(coarse.at[0], coarse_in.at[mu], coarse_send.at[mu], coarse_recv.at[mu], device)
-
-    def hop_copy(mu):
-        return remote(
-            coarse.at[1 + mu], hop_in.at[mu], coarse_send.at[3 + mu], coarse_recv.at[3 + mu], plus[mu]
-        )
-
-    hop_copy(0).start()
-    to_relay = remote(coarse.at[0], relay_in, relay_send.at[0], relay_recv, across)
-    from_relay = remote(relay_in, coarse_in.at[0], relay_send.at[1], coarse_recv.at[0], below)
-
-    @pl.when(low)
-    def _():
-        to_relay.start()
-
-    @pl.when(jnp.logical_not(low))
-    def _():
-        value_copy(0, minus[0]).start()
-
     for mu in (1, 2):
-        value_copy(mu, minus[mu]).start()
+        coarse[1 + mu] = fold(adjoint(split, tops[mu]))
         hop_copy(mu).start()
 
     @pl.when(low)
@@ -223,28 +211,30 @@
         from_relay.start()
         signal(met.at[0], above)
 
-    loaded("td")
     correction = fold(forward(split, tops[3]))
-    for mu in (2, 1, 0):
-        value_copy(mu, minus[mu]).wait_recv()
-        correction += fold(forward(halves(coarse_in[mu]), tops[mu]))
-        hop_copy(mu).wait_recv()
-        correction += hop_in[mu]
+    taken(total.at[pl.ds(0, 4)], coarse_recv.at[1])
+    for mu in (2, 1):
+        correction += fold(forward(halves(coarse_in[mu]), tops[mu])) + hop_in[mu]
+    taken(total.at[pl.ds(0, 2)], coarse_recv.at[0])
+    correction += fold(forward(halves(coarse_in[0]), tops[0])) + hop_in[0]
     coarse_fix = correction.astype(BF16)
 
     def span(part):
         return pl.ds(part * SPAN, SPAN)
+
+    def landing(turn, mu, part):
+        return near_recv.at[turn, mu - 1] if mu else wrap_recv.at[turn, part]
 
     def field_copy(turn, mu, part):
         return remote(
             field[turn].at[span(part)], field_in.at[turn, mu, span(part)],
-            field_send.at[turn, mu, part], field_recv.at[turn, mu, part], minus[mu],
+            field_send, landing(turn, mu, part), minus[mu],
         )
 
     def back_copy(turn, mu, part):
         return remote(
             back.at[turn, mu, span(part)], back_in.at[turn, mu, span(part)],
-            back_send.at[turn, mu, part], back_recv.at[turn, mu, part], plus[mu],
+            field_send, landing(turn, mu, part), plus[mu],
         )
 
     def sites(part):
@@ -263,54 +253,65 @@
             value += adjoint(field[turn][before], links[3, before]).astype(BF16).astype(F32)
             total[n] = value
 
-    def arrived(turn, mu, part):
-        field_copy(turn, mu, part).wait_recv()
-        back_copy(turn, mu, part).wait_recv()
-
     def hop_terms(turn, mu, n):
         return forward(field_in[turn, mu, n], links[mu, n]) + back_in[turn, mu, n].astype(F32)
 
     def near_terms(turn):
         for mu in (2, 1):
-            for part in range(CHUNKS):
-                arrived(turn, mu, part)
-                for n in sites(part):
-                    total[n] += hop_terms(turn, mu, n)
-
-    def send_near(turn):
+            taken(field_in.at[turn, pl.ds(0, 2)], near_recv.at[turn, mu - 1])
+            for n in range(NX):
+                total[n] += hop_terms(turn, mu, n)
+
+    def send_wrap(turn, part):
+        @pl.when(low)
+        def _():
+            field_copy(turn, 0, part).start()
+
+        for n in sites(part):
+            back[turn, 0, n] = adjoint(field[turn][n], links[0, n]).astype(BF16)
+
+        @pl.when(high)
+        def _():
+            back_copy(turn, 0, part).start()
+
+    def send_rest(turn):
         for mu in (1, 2):
             for part in range(CHUNKS):
                 field_copy(turn, mu, part).start()
         for mu in (1, 2):
             for part in range(CHUNKS):
                 send_back(turn, mu, part)
-
-    loaded("lt")
+        for part in range(CHUNKS):
+
+            @pl.when(jnp.logical_not(low))
+            def _():
+                field_copy(turn, 0, part).start()
+
+            @pl.when(jnp.logical_not(high))
+            def _():
+                back_copy(turn, 0, part).start()
+
+    taken(links, load_sem.at[2 * LOADS + 1])
     for part in range(CHUNKS):
         for n in sites(part):
             field[0][n] = forward(coarse_fix, pro[n]).astype(BF16)
-        field_copy(0, 0, part).start()
-        send_back(0, 0, part)
-    loaded("lz")
-    loaded("ly")
-    send_near(0)
+        send_wrap(0, part)
+    send_rest(0)
     pl.semaphore_wait(met.at[0], 2 + jnp.where(jnp.logical_or(low, high), 1, 2))
     for step in ({"y": 2}, {"y": 6}, {"z": 2}, {"z": 6}):
         signal(met.at[1], partner(step))
-    loaded("lx")
-    loaded("diag")
+    taken(diag, load_sem.at[2 * LOADS + 2])
     local_terms(0)
     near_terms(0)
     pl.semaphore_wait(met.at[1], 4)
     signal(met.at[2], across)
     for part in range(CHUNKS):
-        arrived(0, 0, part)
+        taken(field_in.at[0, 0, pl.ds(0, 2 * SPAN)], wrap_recv.at[0, part])
         for n in sites(part):
             applied = total[n] + hop_terms(0, 0, n)
             field[1][n] = (src[n].astype(F32) - applied).astype(BF16)
-        field_copy(1, 0, part).start()
-        send_back(1, 0, part)
-    send_near(1)
+        send_wrap(1, part)
+    send_rest(1)
 
     local_terms(1)
     pl.semaphore_wait(met.at[2], 1)
@@ -323,7 +324,7 @@
     cross = jnp.zeros((RHS, DOF), F32)
     energy = jnp.zeros((RHS, DOF), F32)
     for part in range(CHUNKS):
-        arrived(1, 0, part)
+        taken(field_in.at[1, 0, pl.ds(0, 2 * SPAN)], wrap_recv.at[1, part])
         for n in sites(part):
             value = total[n] + hop_terms(1, 0, n)
             image[n] = value
@@ -342,7 +343,7 @@
 
     def own_copy(slot, depth, step):
         return remote(
-            own, direct_in.at[slot], direct_send.at[depth], direct_recv, partner_at(depth, step)
+            own, direct_in.at[slot], direct_send, direct_recv, partner_at(depth, step)
         )
 
     @pl.when(high)
@@ -360,36 +361,60 @@
 
     def along_copy(slot):
         return remote(
-            own, sum_in.at[slot], sum_send.at[slot], sum_recv.at[slot], partner({"z": slot + 1})
-        )
-
-    def some(slot, hidden, act):
-        if slot < EARLY:
-            pl.when(jnp.logical_not(hidden))(act)
-        else:
-            act()
-
-    for slot in range(7):
-        some(slot, high, lambda: along_copy(slot).start())
-    for slot in range(7):
-        some(slot, z == slot, lambda: along_copy(slot).wait_recv())
+            own, sum_in.at[slot], sum_send, sum_recv.at[0], partner({"z": slot + 1})
+        )
+
+    @pl.when(jnp.logical_not(high))
+    def _():
+        for slot in range(EARLY):
+            along_copy(slot).start()
+
+    for slot in range(EARLY, 7):
+        along_copy(slot).start()
+
+    @pl.when(z < EARLY)
+    def _():
+        taken(sum_in.at[pl.ds(0, 6)], sum_recv.at[0])
+
+    @pl.when(z >= EARLY)
+    def _():
+        taken(sum_in.at[pl.ds(0, 7)], sum_recv.at[0])
+
     for slot in range(7):
         sums = sums + sum_in[slot]
 
     sum_out[1] = sums
     plane_copies = [
-        remote(sum_out.at[1], sum_in.at[7 + slot], sum_send.at[7 + slot], sum_recv.at[7 + slot], partner(step))
+        remote(sum_out.at[1], sum_in.at[7 + slot], sum_send, sum_recv.at[1], partner(step))
         for slot, step in enumerate(offsets_of(("core", "x", "y")))
     ]
     for copy in plane_copies:
         copy.start()
-    for copy in plane_copies:
-        copy.wait_recv()
+    taken(sum_in.at[pl.ds(7, 63)], sum_recv.at[1])
     sums = sums + jnp.sum(sum_in[7:], axis=0)
 
+    @pl.when(low)
+    def _():
+        taken(total.at[pl.ds(0, 7)], coarse_send)
+
+    @pl.when(jnp.logical_not(low))
+    def _():
+        taken(total.at[pl.ds(0, 6)], coarse_send)
+
+    taken(links.at[pl.ds(0, 3)], field_send)
+
+    @pl.when(high)
+    def _():
+        taken(sum_in.at[pl.ds(0, 70 - EARLY)], sum_send)
+        taken(total.at[pl.ds(0, 2 * EARLY)], direct_send)
+
+    @pl.when(jnp.logical_not(high))
+    def _():
+        taken(sum_in, sum_send)
+
     @pl.when(z < EARLY)
     def _():
-        pltpu.make_async_copy(direct_in, direct_in, direct_recv).wait()
+        taken(direct_in, direct_recv)
 
     sums = sums + jnp.sum(direct_in[...], axis=0)
 
@@ -397,35 +422,6 @@
     cross_sum = jnp.sum(jnp.where(lane == row, wide, 0.0), axis=1, keepdims=True)
     energy_sum = jnp.sum(jnp.where(lane == row + RHS, wide, 0.0), axis=1, keepdims=True)
     factor[...] = jnp.broadcast_to(cross_sum / (energy_sum + 1e-06), (RHS, DOF))
-
-    @pl.when(low)
-    def _():
-        to_relay.wait_send()
-        from_relay.wait_send()
-
-    @pl.when(jnp.logical_not(low))
-    def _():
-        value_copy(0, minus[0]).wait_send()
-
-    for mu in range(3):
-        if mu:
-            value_copy(mu, minus[mu]).wait_send()
-        hop_copy(mu).wait_send()
-    for slot in range(7):
-        some(slot, high, lambda: along_copy(slot).wait_send())
-    for copy in plane_copies:
-        copy.wait_send()
-
-    @pl.when(high)
-    def _():
-        for depth in range(EARLY):
-            pltpu.make_async_copy(direct_in, direct_in, direct_send.at[depth]).wait()
-
-    for turn in range(2):
-        for mu in range(3):
-            for part in range(CHUNKS):
-                field_copy(turn, mu, part).wait_send()
-                back_copy(turn, mu, part).wait_send()
 
 
 def body(source, diag_block, link_time, link_zaxis, link_yaxis, link_xaxis, prolong,
@@ -464,19 +460,17 @@
             vmem((2, 1, DOF), F32),
             vmem((total, 1, DOF), F32),
             vmem((64, 1, DOF), F32),
-            dma((2 * LOADS + 9,)),
-            dma((6,)),
-            dma((6,)),
-            dma((2, 3, CHUNKS)),
-            dma((2, 3, CHUNKS)),
-            dma((2, 3, CHUNKS)),
-            dma((2, 3, CHUNKS)),
-            dma((total,)),
-            dma((total,)),
-            dma((EARLY,)),
+            dma((2 * LOADS + 3,)),
+            dma,
+            dma((2,)),
+            dma,
+            dma((2, 2)),
+            dma((2, CHUNKS)),
+            dma,
+            dma((2,)),
+            dma,
             dma,
             vmem((RHS, DOF), F32),
-            dma((2,)),
             dma,
             pltpu.SemaphoreType.REGULAR,
             pltpu.SemaphoreType.REGULAR((4,)),

time: 49.3 us -> 47.4 us (0.961)
  Pallas kernels: 47.7 us -> 45.8 us
    pallas_call x1, Pallas kernels: 47.7 us -> 45.8 us  [body(): pl.pallas_call(kernel, out_shape=(vmem((NX, RHS, DOF), BF16), vmem((NX, R...]
where the time goes in v6:
time: 47.4 us; the launch traced here: 47.3 us
  Pallas kernels  45.8 us (97%)
  other arithmetic  0.79 us (2%)
  between operations  0.64 us (1%)
    pallas_call x1, Pallas kernels, body(): pl.pallas_call(kernel, out_shape=(vmem((NX, RHS, DOF), BF16), vmem((NX, R...  45.8 us

profile of v6, /device:TPU:1, one launch (start us, length us, event | category | flops | bytes accessed | tf_op | source)
XLA Modules:
  0.0 47.3 jit_solution(13037922389053312295)
XLA Ops:
  0.6 45.8 %smooth.1 = (bf16[12,32,128]{2,1,0:T(8,128)(2,1)S(1)}, bf16[12,32,128]{2,1,0:T(8,128)(2,1)S(1)}, f32[12,32,128]{2,1,0:T(8,128)S(1)}, f32[32,128]{1,0:T(8,128)S(1)}) custom-call(bf16[12,32,128]{2,1,0:T(8,128)(2,1)} %bitcast.21, bf16[12,128,128]{2,1,0:T(8,128)(2,1)} %bitcast.15, bf16[12,128,128]{2,1,0:T(8,128)(2,1)} %bitcast.16, ...), custom_call_target="tpu_custom_call" | custom-call | tf_op jit(solution)/shard_map/smooth/pallas_call | solution.py:437
  46.5 0.8 %fusion.2 = (f32[1,1,1,12,32,128]{5,4,3,2,1,0:T(8,128)}, f32[1,1,1,12,32,128]{5,4,3,2,1,0:T(8,128)}) fusion(bf16[12,32,128]{2,1,0:T(8,128)(2,1)S(1)} %get-tuple-element.8, f32[12,32,128]{2,1,0:T(8,128)S(1)} %get-tuple-element.9, f32[32,128]{1,0:T(8,128)S(1)} %get-tuple-element.7, bf16[12,32,128]{2,1,0:T(8,128)(2,1)S(1)} %get-tuple-element.6), kind=kLoop, calls=%fused_computation.4 | loop fusion | flops 294912 | bytes 802816 | tf_op jit(solution)/shard_map/reshape | solution.py:486

commit v7 on v6

--- a/solution.py
+++ b/solution.py
@@ -52,7 +52,7 @@
     back, field_in, back_in, total,
     coarse, coarse_in, hop_in,
     sum_out, sum_in, direct_in,
-    load_sem, coarse_send, coarse_recv, field_send, near_recv, wrap_recv,
+    load_sem, coarse_send, coarse_recv, field_send, wrap_send, near_recv, wrap_recv,
     sum_send, sum_recv, direct_send, direct_recv,
     relay_in, relay_recv, late_in, met,
 ):
@@ -115,9 +115,6 @@
         load(src_h.at[some], src.at[some], 2 * part + 1)
     for slot, source in enumerate((tt_h, tz_h, ty_h, td_h)):
         load(source, tops.at[slot], 2 * LOADS)
-    for slot, source in enumerate((lt_h, lz_h, ly_h, lx_h)):
-        load(source, links.at[slot], 2 * LOADS + 1)
-    load(diag_h, diag, 2 * LOADS + 2)
 
     def signal(semaphore, device):
         pl.semaphore_signal(semaphore, inc=1, device_id=device, device_id_type=MESH)
@@ -157,10 +154,14 @@
         taken(src.at[some], load_sem.at[2 * part + 1])
         for n in range(part * (NX // LOADS), (part + 1) * (NX // LOADS)):
             restricted += adjoint(src[n], pro[n])
-    coarse[0] = restricted
+    coarse[0] = restricted.astype(BF16)
     split = halves(restricted)
+    for slot, source in enumerate((lt_h, lz_h, ly_h, lx_h)):
+        load(source, links.at[slot], 2 * LOADS + 1)
+    load(diag_h, diag, 2 * LOADS + 2)
+
     taken(tops, load_sem.at[2 * LOADS])
-    coarse[1] = fold(adjoint(split, tops[0]))
+    coarse[1] = fold(adjoint(split, tops[0])).astype(BF16)
 
     pl.semaphore_wait(barrier, greetings)
 
@@ -201,7 +202,7 @@
         signal(met.at[0], above)
 
     for mu in (1, 2):
-        coarse[1 + mu] = fold(adjoint(split, tops[mu]))
+        coarse[1 + mu] = fold(adjoint(split, tops[mu])).astype(BF16)
         hop_copy(mu).start()
 
     @pl.when(low)
@@ -212,11 +213,11 @@
         signal(met.at[0], above)
 
     correction = fold(forward(split, tops[3]))
-    taken(total.at[pl.ds(0, 4)], coarse_recv.at[1])
+    taken(back.at[0, 0, pl.ds(0, 4)], coarse_recv.at[1])
     for mu in (2, 1):
-        correction += fold(forward(halves(coarse_in[mu]), tops[mu])) + hop_in[mu]
-    taken(total.at[pl.ds(0, 2)], coarse_recv.at[0])
-    correction += fold(forward(halves(coarse_in[0]), tops[0])) + hop_in[0]
+        correction += forward(coarse_in[mu], tops[mu]) + hop_in[mu].astype(F32)
+    taken(back.at[0, 0, pl.ds(0, 2)], coarse_recv.at[0])
+    correction += forward(coarse_in[0], tops[0]) + hop_in[0].astype(F32)
     coarse_fix = correction.astype(BF16)
 
     def span(part):
@@ -228,7 +229,7 @@
     def field_copy(turn, mu, part):
         return remote(
             field[turn].at[span(part)], field_in.at[turn, mu, span(part)],
-            field_send, landing(turn, mu, part), minus[mu],
+            wrap_send if (turn, mu) == (1, 0) else field_send, landing(turn, mu, part), minus[mu],
         )
 
     def back_copy(turn, mu, part):
@@ -311,6 +312,11 @@
             applied = total[n] + hop_terms(0, 0, n)
             field[1][n] = (src[n].astype(F32) - applied).astype(BF16)
         send_wrap(1, part)
+
+    @pl.when(low)
+    def _():
+        taken(field_in.at[1, 0], wrap_send)
+
     send_rest(1)
 
     local_terms(1)
@@ -395,13 +401,17 @@
 
     @pl.when(low)
     def _():
-        taken(total.at[pl.ds(0, 7)], coarse_send)
+        taken(back.at[0, 0, pl.ds(0, 7)], coarse_send)
 
     @pl.when(jnp.logical_not(low))
     def _():
-        taken(total.at[pl.ds(0, 6)], coarse_send)
-
-    taken(links.at[pl.ds(0, 3)], field_send)
+        taken(back.at[0, 0, pl.ds(0, 6)], coarse_send)
+
+    @pl.when(jnp.logical_not(low))
+    def _():
+        taken(field_in.at[1, 0], wrap_send)
+
+    taken(links.at[pl.ds(0, 3), pl.ds(0, 11)], field_send)
 
     @pl.when(high)
     def _():
@@ -454,9 +464,9 @@
             vmem((2, 3, NX, RHS, DOF), BF16),
             vmem((2, 3, NX, RHS, DOF), BF16),
             vmem((NX, RHS, DOF), F32),
-            vmem((4, RHS, DOF), F32),
-            vmem((3, RHS, DOF), F32),
-            vmem((3, RHS, DOF), F32),
+            vmem((4, RHS, DOF), BF16),
+            vmem((3, RHS, DOF), BF16),
+            vmem((3, RHS, DOF), BF16),
             vmem((2, 1, DOF), F32),
             vmem((total, 1, DOF), F32),
             vmem((64, 1, DOF), F32),
@@ -464,13 +474,14 @@
             dma,
             dma((2,)),
             dma,
+            dma,
             dma((2, 2)),
             dma((2, CHUNKS)),
             dma,
             dma((2,)),
             dma,
             dma,
-            vmem((RHS, DOF), F32),
+            vmem((RHS, DOF), BF16),
             dma,
             pltpu.SemaphoreType.REGULAR,
             pltpu.SemaphoreType.REGULAR((4,)),

time: 47.4 us -> 47 us (level)
  no operation moved by 1% of the time
where the time goes in v7:
time: 47 us; the launch traced here: 46.8 us
  Pallas kernels  45.4 us (97%)
  other arithmetic  0.79 us (2%)
  between operations  0.64 us (1%)
    pallas_call x1, Pallas kernels, body(): pl.pallas_call(kernel, out_shape=(vmem((NX, RHS, DOF), BF16), vmem((NX, R...  45.4 us

profile of v7, /device:TPU:1, one launch (start us, length us, event | category | flops | bytes accessed | tf_op | source)
XLA Modules:
  0.0 46.8 jit_solution(2470008877127513404)
XLA Ops:
  0.6 45.4 %smooth.1 = (bf16[12,32,128]{2,1,0:T(8,128)(2,1)S(1)}, bf16[12,32,128]{2,1,0:T(8,128)(2,1)S(1)}, f32[12,32,128]{2,1,0:T(8,128)S(1)}, f32[32,128]{1,0:T(8,128)S(1)}) custom-call(bf16[12,32,128]{2,1,0:T(8,128)(2,1)} %bitcast.21, bf16[12,128,128]{2,1,0:T(8,128)(2,1)} %bitcast.15, bf16[12,128,128]{2,1,0:T(8,128)(2,1)} %bitcast.16, ...), custom_call_target="tpu_custom_call" | custom-call | tf_op jit(solution)/shard_map/smooth/pallas_call | solution.py:447
  46.0 0.8 %fusion.2 = (f32[1,1,1,12,32,128]{5,4,3,2,1,0:T(8,128)}, f32[1,1,1,12,32,128]{5,4,3,2,1,0:T(8,128)}) fusion(bf16[12,32,128]{2,1,0:T(8,128)(2,1)S(1)} %get-tuple-element.8, f32[12,32,128]{2,1,0:T(8,128)S(1)} %get-tuple-element.9, f32[32,128]{1,0:T(8,128)S(1)} %get-tuple-element.7, bf16[12,32,128]{2,1,0:T(8,128)(2,1)S(1)} %get-tuple-element.6), kind=kLoop, calls=%fused_computation.4 | loop fusion | flops 294912 | bytes 802816 | tf_op jit(solution)/shard_map/reshape | solution.py:497

commit v8 on v6

--- a/solution.py
+++ b/solution.py
@@ -52,7 +52,7 @@
     back, field_in, back_in, total,
     coarse, coarse_in, hop_in,
     sum_out, sum_in, direct_in,
-    load_sem, coarse_send, coarse_recv, field_send, near_recv, wrap_recv,
+    load_sem, coarse_send, coarse_recv, field_send, wrap_send, near_recv, wrap_recv,
     sum_send, sum_recv, direct_send, direct_recv,
     relay_in, relay_recv, late_in, met,
 ):
@@ -115,9 +115,6 @@
         load(src_h.at[some], src.at[some], 2 * part + 1)
     for slot, source in enumerate((tt_h, tz_h, ty_h, td_h)):
         load(source, tops.at[slot], 2 * LOADS)
-    for slot, source in enumerate((lt_h, lz_h, ly_h, lx_h)):
-        load(source, links.at[slot], 2 * LOADS + 1)
-    load(diag_h, diag, 2 * LOADS + 2)
 
     def signal(semaphore, device):
         pl.semaphore_signal(semaphore, inc=1, device_id=device, device_id_type=MESH)
@@ -159,6 +156,10 @@
             restricted += adjoint(src[n], pro[n])
     coarse[0] = restricted
     split = halves(restricted)
+    for slot, source in enumerate((lt_h, lz_h, ly_h, lx_h)):
+        load(source, links.at[slot], 2 * LOADS + 1)
+    load(diag_h, diag, 2 * LOADS + 2)
+
     taken(tops, load_sem.at[2 * LOADS])
     coarse[1] = fold(adjoint(split, tops[0]))
 
@@ -228,7 +229,7 @@
     def field_copy(turn, mu, part):
         return remote(
             field[turn].at[span(part)], field_in.at[turn, mu, span(part)],
-            field_send, landing(turn, mu, part), minus[mu],
+            wrap_send if (turn, mu) == (1, 0) else field_send, landing(turn, mu, part), minus[mu],
         )
 
     def back_copy(turn, mu, part):
@@ -275,10 +276,10 @@
             back_copy(turn, 0, part).start()
 
     def send_rest(turn):
-        for mu in (1, 2):
+        for mu in (2, 1):
             for part in range(CHUNKS):
                 field_copy(turn, mu, part).start()
-        for mu in (1, 2):
+        for mu in (2, 1):
             for part in range(CHUNKS):
                 send_back(turn, mu, part)
         for part in range(CHUNKS):
@@ -311,6 +312,11 @@
             applied = total[n] + hop_terms(0, 0, n)
             field[1][n] = (src[n].astype(F32) - applied).astype(BF16)
         send_wrap(1, part)
+
+    @pl.when(low)
+    def _():
+        taken(field_in.at[1, 0], wrap_send)
+
     send_rest(1)
 
     local_terms(1)
@@ -401,7 +407,11 @@
     def _():
         taken(total.at[pl.ds(0, 6)], coarse_send)
 
-    taken(links.at[pl.ds(0, 3)], field_send)
+    @pl.when(jnp.logical_not(low))
+    def _():
+        taken(field_in.at[1, 0], wrap_send)
+
+    taken(links.at[pl.ds(0, 3), pl.ds(0, 11)], field_send)
 
     @pl.when(high)
     def _():
@@ -464,6 +474,7 @@
             dma,
             dma((2,)),
             dma,
+            dma,
             dma((2, 2)),
             dma((2, CHUNKS)),
             dma,

time: 47.4 us -> 46.9 us (0.989)
  Pallas kernels: 45.8 us -> 45.3 us
    pallas_call x1, Pallas kernels: 45.8 us -> 45.3 us  [body(): pl.pallas_call(kernel, out_shape=(vmem((NX, RHS, DOF), BF16), vmem((NX, R...]
where the time goes in v8:
time: 46.9 us; the launch traced here: 46.7 us
  Pallas kernels  45.3 us (97%)
  other arithmetic  0.79 us (2%)
  between operations  0.64 us (1%)
    pallas_call x1, Pallas kernels, body(): pl.pallas_call(kernel, out_shape=(vmem((NX, RHS, DOF), BF16), vmem((NX, R...  45.3 us

profile of v8, /device:TPU:1, one launch (start us, length us, event | category | flops | bytes accessed | tf_op | source)
XLA Modules:
  0.0 46.7 jit_solution(12509010829599061995)
XLA Ops:
  0.6 45.3 %smooth.1 = (bf16[12,32,128]{2,1,0:T(8,128)(2,1)S(1)}, bf16[12,32,128]{2,1,0:T(8,128)(2,1)S(1)}, f32[12,32,128]{2,1,0:T(8,128)S(1)}, f32[32,128]{1,0:T(8,128)S(1)}) custom-call(bf16[12,32,128]{2,1,0:T(8,128)(2,1)} %bitcast.21, bf16[12,128,128]{2,1,0:T(8,128)(2,1)} %bitcast.15, bf16[12,128,128]{2,1,0:T(8,128)(2,1)} %bitcast.16, ...), custom_call_target="tpu_custom_call" | custom-call | tf_op jit(solution)/shard_map/smooth/pallas_call | solution.py:447
  45.9 0.8 %fusion.2 = (f32[1,1,1,12,32,128]{5,4,3,2,1,0:T(8,128)}, f32[1,1,1,12,32,128]{5,4,3,2,1,0:T(8,128)}) fusion(bf16[12,32,128]{2,1,0:T(8,128)(2,1)S(1)} %get-tuple-element.8, f32[12,32,128]{2,1,0:T(8,128)S(1)} %get-tuple-element.9, f32[32,128]{1,0:T(8,128)S(1)} %get-tuple-element.7, bf16[12,32,128]{2,1,0:T(8,128)(2,1)S(1)} %get-tuple-element.6), kind=kLoop, calls=%fused_computation.4 | loop fusion | flops 294912 | bytes 802816 | tf_op jit(solution)/shard_map/reshape | solution.py:497

commit v9 on v8

--- a/solution.py
+++ b/solution.py
@@ -95,10 +95,6 @@
     across = partner({"y": 4})
     below, above = partner({"z": 7}), partner({"z": 1})
 
-    direct_in[...] = jnp.zeros_like(direct_in)
-    for slot in range(EARLY):
-        sum_in[slot] = jnp.zeros((1, DOF), F32)
-
     def partner_at(depth, step):
         ta_at, gz_at, yx_at = partner(step)
         return at((ta_at // 8) * 8 + depth, gz_at, yx_at)
@@ -115,6 +111,10 @@
         load(src_h.at[some], src.at[some], 2 * part + 1)
     for slot, source in enumerate((tt_h, tz_h, ty_h, td_h)):
         load(source, tops.at[slot], 2 * LOADS)
+
+    direct_in[...] = jnp.zeros_like(direct_in)
+    for slot in range(EARLY):
+        sum_in[slot] = jnp.zeros((1, DOF), F32)
 
     def signal(semaphore, device):
         pl.semaphore_signal(semaphore, inc=1, device_id=device, device_id_type=MESH)
@@ -264,9 +264,11 @@
                 total[n] += hop_terms(turn, mu, n)
 
     def send_wrap(turn, part):
-        @pl.when(low)
-        def _():
-            field_copy(turn, 0, part).start()
+        if turn:
+
+            @pl.when(low)
+            def _():
+                field_copy(turn, 0, part).start()
 
         for n in sites(part):
             back[turn, 0, n] = adjoint(field[turn][n], links[0, n]).astype(BF16)
@@ -296,6 +298,12 @@
     for part in range(CHUNKS):
         for n in sites(part):
             field[0][n] = forward(coarse_fix, pro[n]).astype(BF16)
+
+        @pl.when(low)
+        def _():
+            field_copy(0, 0, part).start()
+
+    for part in range(CHUNKS):
         send_wrap(0, part)
     send_rest(0)
     pl.semaphore_wait(met.at[0], 2 + jnp.where(jnp.logical_or(low, high), 1, 2))

time: 46.9 us -> 47.1 us (level)
  no operation moved by 1% of the time
where the time goes in v9:
time: 47.1 us; the launch traced here: 47 us
  Pallas kernels  45.6 us (97%)
  other arithmetic  0.79 us (2%)
  between operations  0.64 us (1%)
    pallas_call x1, Pallas kernels, body(): pl.pallas_call(kernel, out_shape=(vmem((NX, RHS, DOF), BF16), vmem((NX, R...  45.6 us

profile of v9, /device:TPU:1, one launch (start us, length us, event | category | flops | bytes accessed | tf_op | source)
XLA Modules:
  0.0 47.0 jit_solution(17458768464775661440)
XLA Ops:
  0.6 45.6 %smooth.1 = (bf16[12,32,128]{2,1,0:T(8,128)(2,1)S(1)}, bf16[12,32,128]{2,1,0:T(8,128)(2,1)S(1)}, f32[12,32,128]{2,1,0:T(8,128)S(1)}, f32[32,128]{1,0:T(8,128)S(1)}) custom-call(bf16[12,32,128]{2,1,0:T(8,128)(2,1)} %bitcast.21, bf16[12,128,128]{2,1,0:T(8,128)(2,1)} %bitcast.15, bf16[12,128,128]{2,1,0:T(8,128)(2,1)} %bitcast.16, ...), custom_call_target="tpu_custom_call" | custom-call | tf_op jit(solution)/shard_map/smooth/pallas_call | solution.py:455
  46.2 0.8 %fusion.2 = (f32[1,1,1,12,32,128]{5,4,3,2,1,0:T(8,128)}, f32[1,1,1,12,32,128]{5,4,3,2,1,0:T(8,128)}) fusion(bf16[12,32,128]{2,1,0:T(8,128)(2,1)S(1)} %get-tuple-element.8, f32[12,32,128]{2,1,0:T(8,128)S(1)} %get-tuple-element.9, f32[32,128]{1,0:T(8,128)S(1)} %get-tuple-element.7, bf16[12,32,128]{2,1,0:T(8,128)(2,1)S(1)} %get-tuple-element.6), kind=kLoop, calls=%fused_computation.4 | loop fusion | flops 294912 | bytes 802816 | tf_op jit(solution)/shard_map/reshape | solution.py:505
